TPU v7x, 32 devices: a whole 2x2x4 slice. The times are simulated.
32 devices in a mesh: dp: 8 (over y, x, core), seq: 4 (over z).
Axes of the slice: x: 2, y: 2, z: 4, core: 2. Of those that a mesh axis runs over, the one named last changes fastest.
Arguments:
- inputs: bfloat16 [8, 1, 5120, 512], P('dp', None, 'seq'), may hold values from -6 to 6
- lengths: int32 [8, 1, 3], P('dp'), may hold values from 0 to 3072, as said below
- cotangent: bfloat16 [8, 1, 5120, 512], P('dp', None, 'seq'), may hold values from -6 to 6
- gain_one: bfloat16 [512], P('dp'), may hold values from 0.5 to 1.5
- shift_one: bfloat16 [512], P('dp'), may hold values from -3 to 3
- w_qkv: bfloat16 [512, 1536], P('dp'), may hold values from -0.25 to 0.25
- b_qk: bfloat16 [1024], P('dp'), may hold values from -3 to 3
- w_out: bfloat16 [512, 512], P('dp'), may hold values from -2 to 2
- b_out: bfloat16 [512], P('dp'), may hold values from -3 to 3
- gain_two: bfloat16 [512], P('dp'), may hold values from 0.5 to 1.5
- shift_two: bfloat16 [512], P('dp'), may hold values from -3 to 3
- w_up: bfloat16 [512, 2048], P('dp'), may hold values from -0.25 to 0.25
- b_up: bfloat16 [2048], P('dp'), may hold values from -3 to 3
- w_down: bfloat16 [2048, 512], P('dp'), may hold values from -0.125 to 0.125
- b_down: bfloat16 [512], P('dp'), may hold values from -3 to 3
Outputs:
- outputs: bfloat16 [8, 1, 5120, 512], P('dp', None, 'seq')
- grad_inputs: float32 [8, 1, 5120, 512], P('dp', None, 'seq')
- grad_gain_one: float32 [512], P('dp')
- grad_shift_one: float32 [512], P('dp')
- grad_w_qkv: float32 [512, 1536], P('dp')
- grad_b_qk: float32 [1024], P('dp')
- grad_w_out: float32 [512, 512], P('dp')
- grad_b_out: float32 [512], P('dp')
- grad_gain_two: float32 [512], P('dp')
- grad_shift_two: float32 [512], P('dp')
- grad_w_up: float32 [512, 2048], P('dp')
- grad_b_up: float32 [2048], P('dp')
- grad_w_down: float32 [2048, 512], P('dp')
- grad_b_down: float32 [512], P('dp')
Inputs may be any that keep to these rules, and one draw needn't show every extreme that they name: `lengths`: each pack holds an image of 784 rows, then one of 3072 rows, then either another of 784 rows or none (length 0); the rest of the pack is one more segment.
All inputs are finite; a program needn't handle non-finite values.
Results may differ from a plain program's by a relative error of at most 0.03.
The roundings to bfloat16 on the way count: a program that leaves them out, or rounds other values in their place, can miss the bound.
Values may be sent and summed in bfloat16 or wider, within the bound.
A program may use at most 192 MiB of HBM per device.

v0:
```python
import jax
import jax.numpy as jnp
from jax import lax
from jax.sharding import PartitionSpec as P

HEADS = 8
BLOCK = 640


highest = lax.Precision.HIGHEST
eps_norm = 1e-05
eps_attn = 1e-06


def entering(value, axis, join, neutral, backward):
    count, mine = (lax.axis_size(axis), lax.axis_index(axis))
    pieces = jax.tree.map(lambda part: lax.all_gather(part, axis), value)
    if backward:
        pieces = jax.tree.map(lambda part: part[::-1], pieces)
        mine = count - 1 - mine
    total = jax.tree.map(
        lambda part, zero: jnp.full_like(part, 0) + jnp.asarray(zero, part.dtype), value, neutral
    )

    def lap(position, total):
        longer = join(total, jax.tree.map(lambda part: part[position], pieces))
        return jax.tree.map(lambda new, old: jnp.where(position < mine, new, old), longer, total)

    return lax.fori_loop(0, count - 1, lap, total)


def norm_layer(values, scale_gain, scale_shift):
    row_mean = jnp.mean(values, axis=-1, keepdims=True)
    centred = values - row_mean
    variance = jnp.mean(centred * centred, axis=-1, keepdims=True)
    return centred * lax.rsqrt(variance + eps_norm) * scale_gain + scale_shift


def feature(values):
    return jax.nn.elu(values) + 1.0


def gelu_exact(values):
    return jax.nn.gelu(values, approximate=False)


def segment_ids(lengths_row, positions):
    bounds = jnp.cumsum(lengths_row)
    return jnp.sum((positions[:, None] >= bounds[None, :]).astype(jnp.int32), axis=1)


def link_maps(earlier, later):
    return (
        later[0] + later[2][:, None, None, None] * earlier[0],
        later[1] + later[2][:, None, None] * earlier[1],
        earlier[2] * later[2],
    )


def block_scores(query_rows, key_rows, segments):
    positions = jnp.arange(segments.shape[0], dtype=jnp.int32)
    visible = (positions[None, :] <= positions[:, None]) & (segments[:, None] == segments[None, :])
    products = jnp.einsum("ihe,jhe->hij", query_rows, key_rows, preferred_element_type=jnp.float32)
    return (jnp.where(visible[None], products, 0.0), visible)


def attend_forward(
    query_rows, key_rows, value_rows, segments, segment_before, key_state, key_total
):
    row_count, head_count, head_size = query_rows.shape
    block_count = row_count // BLOCK

    def blocks(array):
        return array.reshape((block_count, BLOCK) + array.shape[1:])

    def advance(carried, items):
        state_now, total_now, carry_segment = carried
        query_block, key_block, value_block, segment_block = items
        scores, _ = block_scores(query_block, key_block, segment_block)
        alive_rows = (segment_block == carry_segment).astype(jnp.float32)
        query_wide = query_block.astype(jnp.float32)
        within = jnp.einsum(
            "hij,jhf->ihf",
            scores.astype(jnp.bfloat16),
            value_block,
            preferred_element_type=jnp.float32,
        )
        before = jnp.einsum("ihe,hef->ihf", query_wide, state_now, precision=highest)
        numerator = within + alive_rows[:, None, None] * before
        denominator = (
            jnp.sum(scores, axis=2).T
            + alive_rows[:, None]
            * jnp.einsum("ihe,he->ih", query_wide, total_now, precision=highest)
            + eps_attn
        )
        result = numerator / denominator[:, :, None]
        last_segment = segment_block[-1]
        keeping = (last_segment == carry_segment).astype(jnp.float32)
        chosen = segment_block == last_segment
        picked = jnp.where(chosen[:, None, None], value_block, jnp.zeros_like(value_block))
        state_next = keeping * state_now + jnp.einsum(
            "jhe,jhf->hef", key_block, picked, preferred_element_type=jnp.float32
        )
        total_next = keeping * total_now + jnp.einsum(
            "jhe,j->he",
            key_block.astype(jnp.float32),
            chosen.astype(jnp.float32),
            precision=highest,
        )
        return (
            (state_next, total_next, last_segment),
            (result, denominator, state_now, total_now, carry_segment),
        )

    items = (blocks(query_rows), blocks(key_rows), blocks(value_rows), blocks(segments))
    _, stacked = lax.scan(advance, (key_state, key_total, segment_before), items)
    result, denominator, states, totals, carries = stacked
    return (
        result.reshape(row_count, head_count, head_size),
        denominator.reshape(row_count, head_count),
        (states, totals, carries),
    )


def attend_backward(
    query_rows,
    key_rows,
    value_rows,
    segments,
    kept_states,
    result,
    denominator,
    grad_heard,
    grad_state,
    grad_total,
):
    row_count, head_count, head_size = query_rows.shape
    block_count = row_count // BLOCK

    def blocks(array):
        return array.reshape((block_count, BLOCK) + array.shape[1:])

    states, totals, carries = kept_states

    def retreat(carried, items):
        state_grad, total_grad = carried
        (
            query_block,
            key_block,
            value_block,
            segment_block,
            result_block,
            denominator_block,
            grad_block,
            state_now,
            total_now,
            carry_segment,
        ) = items
        scores, visible = block_scores(query_block, key_block, segment_block)
        alive_rows = (segment_block == carry_segment).astype(jnp.float32)
        grad_wide = grad_block.astype(jnp.float32)
        numerator_grad = (grad_wide / denominator_block[:, :, None]).astype(jnp.bfloat16)
        denominator_grad = -jnp.sum(grad_wide * result_block, axis=2) / denominator_block
        numerator_wide = numerator_grad.astype(jnp.float32)
        query_wide = query_block.astype(jnp.float32)
        key_wide = key_block.astype(jnp.float32)
        value_wide = value_block.astype(jnp.float32)
        score_grad = jnp.einsum(
            "ihf,jhf->hij", numerator_grad, value_block, preferred_element_type=jnp.float32
        )
        score_grad = jnp.where(
            visible[None], score_grad + denominator_grad.T[:, :, None], 0.0
        ).astype(jnp.bfloat16)
        value_grad = jnp.einsum(
            "hij,ihf->jhf",
            scores.astype(jnp.bfloat16),
            numerator_grad,
            preferred_element_type=jnp.float32,
        )
        query_grad = jnp.einsum(
            "hij,jhe->ihe", score_grad, key_block, preferred_element_type=jnp.float32
        )
        query_grad = query_grad + alive_rows[:, None, None] * (
            jnp.einsum("ihf,hef->ihe", numerator_wide, state_now, precision=highest)
            + denominator_grad[:, :, None] * total_now[None]
        )
        key_grad = jnp.einsum(
            "hij,ihe->jhe", score_grad, query_block, preferred_element_type=jnp.float32
        )
        last_segment = segment_block[-1]
        keeping = (last_segment == carry_segment).astype(jnp.float32)
        chosen = (segment_block == last_segment).astype(jnp.float32)
        key_grad = key_grad + chosen[:, None, None] * (
            jnp.einsum("jhf,hef->jhe", value_wide, state_grad, precision=highest) + total_grad[None]
        )
        value_grad = value_grad + chosen[:, None, None] * jnp.einsum(
            "jhe,hef->jhf", key_wide, state_grad, precision=highest
        )
        alive_queries = query_wide * alive_rows[:, None, None]
        state_prior = keeping * state_grad + jnp.einsum(
            "ihe,ihf->hef", alive_queries, numerator_wide, precision=highest
        )
        total_prior = keeping * total_grad + jnp.einsum(
            "ihe,ih->he", alive_queries, denominator_grad, precision=highest
        )
        return ((state_prior, total_prior), (query_grad, key_grad, value_grad))

    items = (
        blocks(query_rows),
        blocks(key_rows),
        blocks(value_rows),
        blocks(segments),
        blocks(result),
        blocks(denominator),
        blocks(grad_heard),
        states,
        totals,
        carries,
    )
    _, grad_parts = lax.scan(retreat, (grad_state, grad_total), items, reverse=True)
    return tuple(
        (
            array.reshape(row_count, head_count * head_size).astype(jnp.bfloat16)
            for array in grad_parts
        )
    )


def body(
    inputs,
    lengths,
    cotangent,
    gain_one,
    shift_one,
    w_qkv,
    b_qk,
    w_out,
    b_out,
    gain_two,
    shift_two,
    w_up,
    b_up,
    w_down,
    b_down,
):
    attn_set = (
        lax.all_gather(gain_one, "dp", axis=0, tiled=True),
        lax.all_gather(shift_one, "dp", axis=0, tiled=True),
        lax.all_gather(w_qkv, "dp", axis=0, tiled=True),
        lax.all_gather(b_qk, "dp", axis=0, tiled=True),
        lax.all_gather(w_out, "dp", axis=0, tiled=True),
        lax.all_gather(b_out, "dp", axis=0, tiled=True),
    )
    ffn_set = (
        lax.all_gather(gain_two, "dp", axis=0, tiled=True),
        lax.all_gather(shift_two, "dp", axis=0, tiled=True),
        lax.all_gather(w_up, "dp", axis=0, tiled=True),
        lax.all_gather(b_up, "dp", axis=0, tiled=True),
        lax.all_gather(w_down, "dp", axis=0, tiled=True),
        lax.all_gather(b_down, "dp", axis=0, tiled=True),
    )
    norm_gain, norm_shift, weight_qkv, bias_qk, weight_out, bias_out = attn_set
    gain_later, shift_later, weight_up, bias_up, weight_down, bias_down = ffn_set
    pack_count, row_count, model_width = (inputs.shape[1], inputs.shape[2], inputs.shape[3])
    head_size = model_width // HEADS
    first_row = lax.axis_index("seq") * row_count
    token_count = pack_count * row_count
    flat_inputs = inputs.reshape(token_count, model_width).astype(jnp.float32)
    lengths_here = lengths[0]
    many_segments = jax.vmap(segment_ids, in_axes=(0, None))
    normed, norm_pullback = jax.vjp(
        norm_layer, flat_inputs, norm_gain.astype(jnp.float32), norm_shift.astype(jnp.float32)
    )
    normed_low = normed.astype(jnp.bfloat16)
    bias_full = jnp.concatenate(
        [bias_qk.astype(jnp.float32), jnp.zeros((model_width,), jnp.float32)]
    )
    mixed_pre = jnp.dot(normed_low, weight_qkv, preferred_element_type=jnp.float32) + bias_full
    features, feature_pullback = jax.vjp(feature, mixed_pre[:, : 2 * model_width])
    query_low = features[:, :model_width].astype(jnp.bfloat16)
    key_low = features[:, model_width:].astype(jnp.bfloat16)
    value_low = mixed_pre[:, 2 * model_width :].astype(jnp.bfloat16)
    positions = first_row + jnp.arange(row_count, dtype=jnp.int32)
    segments = many_segments(lengths_here, positions)
    prior_segment = many_segments(lengths_here, positions[:1] - 1)[:, 0]
    prior_segment = jnp.where(first_row > 0, prior_segment, -1)
    head_rows = tuple(
        (
            array.reshape(pack_count, row_count, HEADS, head_size)
            for array in (query_low, key_low, value_low)
        )
    )
    last_segment = segments[:, -1]
    chosen = segments == last_segment[:, None]
    picked = jnp.where(chosen[:, :, None, None], head_rows[2], jnp.zeros_like(head_rows[2]))
    tail_state = jnp.einsum(
        "prhe,prhf->phef", head_rows[1], picked, preferred_element_type=jnp.float32
    )
    tail_total = jnp.einsum(
        "prhe,pr->phe",
        head_rows[1].astype(jnp.float32),
        chosen.astype(jnp.float32),
        precision=highest,
    )
    passing = (prior_segment == last_segment).astype(jnp.float32)
    carry_state, carry_total, _ = entering(
        (tail_state, tail_total, passing),
        "seq",
        link_maps,
        (jnp.zeros_like(tail_state), jnp.zeros_like(tail_total), jnp.ones_like(passing)),
        False,
    )

    def forward_pack(items):
        return attend_forward(items[0], items[1], items[2], items[3], items[4], items[5], items[6])

    result, denominator, kept_states = lax.map(
        forward_pack, head_rows + (segments, prior_segment, carry_state, carry_total)
    )
    heard_low = result.reshape(token_count, model_width).astype(jnp.bfloat16)
    middle = (
        flat_inputs
        + jnp.dot(heard_low, weight_out, preferred_element_type=jnp.float32)
        + bias_out.astype(jnp.float32)
    )
    normed_two, norm_two_pullback = jax.vjp(
        norm_layer, middle, gain_later.astype(jnp.float32), shift_later.astype(jnp.float32)
    )
    normed_two_low = normed_two.astype(jnp.bfloat16)
    hidden = jnp.dot(
        normed_two_low, weight_up, preferred_element_type=jnp.float32
    ) + bias_up.astype(jnp.float32)
    activated, gelu_pullback = jax.vjp(gelu_exact, hidden)
    active_low = activated.astype(jnp.bfloat16)
    produced = (
        middle
        + jnp.dot(active_low, weight_down, preferred_element_type=jnp.float32)
        + bias_down.astype(jnp.float32)
    )
    outputs = produced.astype(jnp.bfloat16).reshape(inputs.shape)
    grad_out = cotangent.reshape(token_count, model_width).astype(jnp.float32)
    branch_grad = grad_out.astype(jnp.bfloat16)
    grad_w_down = jnp.einsum(
        "nf,nd->fd", active_low, branch_grad, preferred_element_type=jnp.float32
    )
    grad_b_down = jnp.sum(branch_grad.astype(jnp.float32), axis=0)
    active_grad = jnp.einsum(
        "nd,fd->nf", branch_grad, weight_down, preferred_element_type=jnp.float32
    )
    hidden_grad = gelu_pullback(active_grad)[0].astype(jnp.bfloat16)
    grad_w_up = jnp.einsum(
        "nd,nf->df", normed_two_low, hidden_grad, preferred_element_type=jnp.float32
    )
    grad_b_up = jnp.sum(hidden_grad.astype(jnp.float32), axis=0)
    normed_two_grad = jnp.einsum(
        "nf,df->nd", hidden_grad, weight_up, preferred_element_type=jnp.float32
    )
    middle_part, grad_gain_two, grad_shift_two = norm_two_pullback(normed_two_grad)
    middle_grad = grad_out + middle_part
    attn_grad = middle_grad.astype(jnp.bfloat16)
    grad_w_out = jnp.einsum("nd,ne->de", heard_low, attn_grad, preferred_element_type=jnp.float32)
    grad_b_out = jnp.sum(attn_grad.astype(jnp.float32), axis=0)
    heard_grad = jnp.einsum(
        "ne,de->nd", attn_grad, weight_out, preferred_element_type=jnp.float32
    ).astype(jnp.bfloat16)
    grad_heads = heard_grad.reshape(pack_count, row_count, HEADS, head_size)
    grad_wide = grad_heads.astype(jnp.float32)
    numerator_grad = (grad_wide / denominator[..., None]).astype(jnp.bfloat16).astype(jnp.float32)
    denominator_grad = -jnp.sum(grad_wide * result, axis=3) / denominator
    alive_rows = (segments == prior_segment[:, None]).astype(jnp.float32)
    alive_queries = head_rows[0].astype(jnp.float32) * alive_rows[:, :, None, None]
    own_state = jnp.einsum("prhe,prhf->phef", alive_queries, numerator_grad, precision=highest)
    own_total = jnp.einsum("prhe,prh->phe", alive_queries, denominator_grad, precision=highest)
    later_state, later_total, _ = entering(
        (own_state, own_total, passing),
        "seq",
        link_maps,
        (jnp.zeros_like(own_state), jnp.zeros_like(own_total), jnp.ones_like(passing)),
        True,
    )

    def backward_pack(items):
        return attend_backward(
            items[0],
            items[1],
            items[2],
            items[3],
            items[4],
            items[5],
            items[6],
            items[7],
            items[8],
            items[9],
        )

    back_parts = lax.map(
        backward_pack,
        head_rows
        + (segments, kept_states, result, denominator, grad_heads, later_state, later_total),
    )
    query_back, key_back, value_back = back_parts
    query_back = query_back.reshape(token_count, model_width)
    key_back = key_back.reshape(token_count, model_width)
    value_back = value_back.reshape(token_count, model_width)
    feature_grad = feature_pullback(
        jnp.concatenate([query_back, key_back], axis=1).astype(jnp.float32)
    )[0]
    mixed_grad = jnp.concatenate([feature_grad, value_back.astype(jnp.float32)], axis=1).astype(
        jnp.bfloat16
    )
    grad_w_qkv = jnp.einsum("nd,nf->df", normed_low, mixed_grad, preferred_element_type=jnp.float32)
    grad_b_qk = jnp.sum(mixed_grad[:, : 2 * model_width].astype(jnp.float32), axis=0)
    normed_grad = jnp.einsum(
        "nf,df->nd", mixed_grad, weight_qkv, preferred_element_type=jnp.float32
    )
    input_part, grad_gain_one, grad_shift_one = norm_pullback(normed_grad)
    input_grad = middle_grad + input_part
    summed = (
        lax.psum(grad_gain_one.astype(jnp.bfloat16), "seq").astype(jnp.float32),
        lax.psum(grad_shift_one.astype(jnp.bfloat16), "seq").astype(jnp.float32),
        lax.psum(grad_w_qkv.astype(jnp.bfloat16), "seq").astype(jnp.float32),
        lax.psum(grad_b_qk.astype(jnp.bfloat16), "seq").astype(jnp.float32),
        lax.psum(grad_w_out.astype(jnp.bfloat16), "seq").astype(jnp.float32),
        lax.psum(grad_b_out.astype(jnp.bfloat16), "seq").astype(jnp.float32),
        lax.psum(grad_gain_two.astype(jnp.bfloat16), "seq").astype(jnp.float32),
        lax.psum(grad_shift_two.astype(jnp.bfloat16), "seq").astype(jnp.float32),
        lax.psum(grad_w_up.astype(jnp.bfloat16), "seq").astype(jnp.float32),
        lax.psum(grad_b_up.astype(jnp.bfloat16), "seq").astype(jnp.float32),
        lax.psum(grad_w_down.astype(jnp.bfloat16), "seq").astype(jnp.float32),
        lax.psum(grad_b_down.astype(jnp.bfloat16), "seq").astype(jnp.float32),
    )
    shards = (
        lax.psum_scatter(
            summed[0].astype(jnp.bfloat16), "dp", scatter_dimension=0, tiled=True
        ).astype(jnp.float32),
        lax.psum_scatter(
            summed[1].astype(jnp.bfloat16), "dp", scatter_dimension=0, tiled=True
        ).astype(jnp.float32),
        lax.psum_scatter(
            summed[2].astype(jnp.bfloat16), "dp", scatter_dimension=0, tiled=True
        ).astype(jnp.float32),
        lax.psum_scatter(
            summed[3].astype(jnp.bfloat16), "dp", scatter_dimension=0, tiled=True
        ).astype(jnp.float32),
        lax.psum_scatter(
            summed[4].astype(jnp.bfloat16), "dp", scatter_dimension=0, tiled=True
        ).astype(jnp.float32),
        lax.psum_scatter(
            summed[5].astype(jnp.bfloat16), "dp", scatter_dimension=0, tiled=True
        ).astype(jnp.float32),
        lax.psum_scatter(
            summed[6].astype(jnp.bfloat16), "dp", scatter_dimension=0, tiled=True
        ).astype(jnp.float32),
        lax.psum_scatter(
            summed[7].astype(jnp.bfloat16), "dp", scatter_dimension=0, tiled=True
        ).astype(jnp.float32),
        lax.psum_scatter(
            summed[8].astype(jnp.bfloat16), "dp", scatter_dimension=0, tiled=True
        ).astype(jnp.float32),
        lax.psum_scatter(
            summed[9].astype(jnp.bfloat16), "dp", scatter_dimension=0, tiled=True
        ).astype(jnp.float32),
        lax.psum_scatter(
            summed[10].astype(jnp.bfloat16), "dp", scatter_dimension=0, tiled=True
        ).astype(jnp.float32),
        lax.psum_scatter(
            summed[11].astype(jnp.bfloat16), "dp", scatter_dimension=0, tiled=True
        ).astype(jnp.float32),
    )
    return (
        outputs,
        input_grad.reshape(inputs.shape),
        shards[0],
        shards[1],
        shards[2],
        shards[3],
        shards[4],
        shards[5],
        shards[6],
        shards[7],
        shards[8],
        shards[9],
        shards[10],
        shards[11],
    )


def solution(mesh):
    in_specs = (
        P("dp", None, "seq", None),
        P("dp", None, None),
        P("dp", None, "seq", None),
        P("dp"),
        P("dp"),
        P("dp", None),
        P("dp"),
        P("dp", None),
        P("dp"),
        P("dp"),
        P("dp"),
        P("dp", None),
        P("dp"),
        P("dp", None),
        P("dp"),
    )
    out_specs = (
        P("dp", None, "seq", None),
        P("dp", None, "seq", None),
        P("dp"),
        P("dp"),
        P("dp", None),
        P("dp"),
        P("dp", None),
        P("dp"),
        P("dp"),
        P("dp"),
        P("dp", None),
        P("dp"),
        P("dp", None),
        P("dp"),
    )
    return jax.shard_map(body, mesh=mesh, in_specs=in_specs, out_specs=out_specs, check_vma=False)
```

profile of v0, /device:TPU:0, one launch (start us, length us, event | category | flops | bytes accessed | tf_op | source)
XLA Modules:
  0.0 624.3 jit_solution(12825425180359258220)
XLA Ops:
  15.9 15.5 %all-reduce.17 = (bf16[512]{0:T(512)(128)(2,1)S(1)}, bf16[512]{0:T(512)(128)(2,1)S(1)}, bf16[512]{0:T(512)(128)(2,1)S(1)}, bf16[512]{0:T(512)(128)(2,1)S(1)}, bf16[512]{0:T(512)(128)(2,1)S(1)}) all-reduce(bf16[512]{0:T(512)(128)(2,1)S(1)} %dynamic-update-slice.1, ...), channel_id=1, replica_groups=mesh['dp'=8,'seq'=4] {'dp'}, use_global_device_ids=true, to_apply=%add.2 | all-reduce | flops 2560 | bytes 10240
  33.9 7.7 %all-gather.5 = bf16[8,1,128]{2,1,0:T(2,128)(2,1)S(1)} all-gather(bf16[1,1,128]{2,1,0:T(2,128)(2,1)S(1)} %bitcast.542), channel_id=1, replica_groups=mesh['dp'=8,'seq'=4] {'dp'}, dimensions={0}, use_global_device_ids=true | all-gather | bytes 2304 | tf_op jit(solution)/shard_map/all_gather | solution.py:250
  47.4 12.5 %all-reduce.3 = f32[4]{0:T(128)} all-reduce(f32[4]{0:T(128)S(1)} %fusion.165), channel_id=3, replica_groups=mesh['dp'=8,'seq'=4] {'seq'}, use_global_device_ids=true, to_apply=%add.3 | all-reduce | flops 4 | bytes 32
  59.9 10.5 %all_gather.82 = bf16[512,512]{1,0:T(8,128)(2,1)S(1)} all-gather(bf16[64,512]{1,0:T(8,128)(2,1)} %param.30), channel_id=1, replica_groups=mesh['dp'=8,'seq'=4] {'dp'}, dimensions={0}, use_global_device_ids=true | all-gather | bytes 589824 | tf_op jit(solution)/shard_map/all_gather | solution.py:251
  70.4 8.2 %all-gather.6 = bf16[8,1,256]{2,1,0:T(2,128)(2,1)S(1)} all-gather(bf16[1,1,256]{2,1,0:T(2,128)(2,1)S(1)} %reshape.584), channel_id=1, replica_groups=mesh['dp'=8,'seq'=4] {'dp'}, dimensions={0}, use_global_device_ids=true | all-gather | bytes 4608 | tf_op jit(solution)/shard_map/all_gather | solution.py:258
  97.2 21.9 %all-gather = f32[32,64,64]{2,1,0:T(8,128)S(1)} all-gather(f32[8,64,64]{2,1,0:T(8,128)S(1)} %fusion.155), channel_id=2, replica_groups=mesh['dp'=8,'seq'=4] {'seq'}, dimensions={0}, use_global_device_ids=true | all-gather | bytes 655360 | tf_op jit(solution)/shard_map/all_gather | solution.py:17
  119.7 13.3 %all-gather.2 = f32[32,64]{1,0:T(8,128)S(1)} all-gather(f32[8,64]{1,0:T(8,128)S(1)} %bitcast.537), channel_id=4, replica_groups=mesh['dp'=8,'seq'=4] {'seq'}, dimensions={0}, use_global_device_ids=true | all-gather | bytes 10240 | tf_op jit(solution)/shard_map/all_gather | solution.py:17
  133.0 6.3 %while.110 = (s32[]{:T(128)}, f32[1,8,64,64]{3,2,1,0:T(8,128)S(1)}, f32[1,8,64]{2,1,0:T(8,128)S(1)}, s32[]{:T(128)}, f32[4,1,8,64,64]{4,3,2,1,0:T(8,128)S(1)}, /...) while((s32[]{:T(128)}, f32[1,8,64,64]{3,2,1,0:T(8,128)S(1)}, ...), condition=%wide.region_6.7_spmd.clone.clone, body=%wide.region_5.6_spmd.clone.sunk.clone | while | flops 133124 | bytes 399487 | solution.py:29
  149.4 29.8 %while.108 = (s32[]{:T(128)}, f32[8,64,64]{2,1,0:T(8,128)S(1)}, f32[8,64]{1,0:T(8,128)S(1)}, s32[]{:T(128)}, f32[2,640,8,64]{1,3,2,0:T(8,128)}, /*index=5*/f32[2...) while((s32[]{:T(128)}, f32[8,64,64]{2,1,0:T(8,128)S(1)}, ...), condition=%wide.region_9.10_spmd.clone, body=%wide.region_7.9_spmd.sunk.clone | while | flops 1152791040 | bytes 30040440 | solution.py:116
  189.2 30.4 %multiply_convert_fusion = (bf16[1280,2048]{1,0:T(8,128)(2,1)}, f32[1280,2048]{1,0:T(8,128)}, f32[1280,2048]{1,0:T(8,128)}) fusion(f32[2048]{0:T(1024)S(1)} %bitcast.540, bf16[512,2048]{1,0:T(8,128)(2,1)} %all-gather.13.cloned.1.call-done, f32[1280,512]{0,1:T(8,128)} %copy-done.8, f32[512]{0:T(512)S(1)} %convert_element_type.366, ...), kind=kOutput, calls=%fused_computation.146 | convolution fusion | flops 2860646400 | bytes 30955520 | tf_op jit(solution)/shard_map/dot_general | solution.py:330
  219.6 12.1 %fusion.183 = (bf16[2048]{0:T(1024)(128)(2,1)}, bf16[1280,2048]{1,0:T(8,128)(2,1)S(1)}) fusion(f32[1280,2048]{1,0:T(8,128)} %get-tuple-element.1121, bf16[2048,512]{1,0:T(8,128)(2,1)} %all-gather.15.cloned.1.call-done, bf16[1,1,1280,512]{3,2,1,0:T(8,128)(2,1)S(1)} %copy-done.19, f32[1280,2048]{1,0:T(8,128)} %get-tuple-element.1140, f32[2048]{0:T(1024)S(1)} %bitcast.541), kind=kOutput, calls=%fused_computation.260 | convolution fusion | flops 2726295552 | bytes 29634560 | tf_op jit(solution)/shard_map/nd,fd->nf/dot_general | solution.py:347
  261.8 13.1 %all-gather.4 = f32[32,64]{1,0:T(8,128)S(1)} all-gather(f32[8,64]{1,0:T(8,128)S(1)} %bitcast.538), channel_id=6, replica_groups=mesh['dp'=8,'seq'=4] {'seq'}, dimensions={0}, use_global_device_ids=true | all-gather | bytes 10240 | tf_op jit(solution)/shard_map/all_gather | solution.py:17
  278.3 19.3 %all-gather.3 = f32[32,64,64]{2,1,0:T(8,128)} all-gather(f32[8,64,64]{2,1,0:T(8,128)S(1)} %fusion.146), channel_id=5, replica_groups=mesh['dp'=8,'seq'=4] {'seq'}, dimensions={0}, use_global_device_ids=true | all-gather | bytes 655360 | tf_op jit(solution)/shard_map/all_gather | solution.py:17
  300.1 9.2 %while.111 = (s32[]{:T(128)}, f32[1,8,64,64]{3,2,1,0:T(8,128)S(1)}, f32[1,8,64]{2,1,0:T(8,128)S(1)}, s32[]{:T(128)}, f32[4,1,8,64,64]{4,3,2,1,0:T(8,128)}, /*index=5*/f32[4,1]{0,1:T(1,128)S(1)}, f32[4,1,8,64]{3,2,1,0:T(8,128)S(1)}) while((s32[]{:T(128)}, f32[1,8,64,64]{3,2,1,0:T(8,128)S(1)}, ...), condition=%wide.region_16.17_spmd.clone.clone, body=%wide.region_15.16_spmd.clone.sunk.clone | while | flops 133124 | bytes 399487 | solution.py:29
  309.3 72.7 %while.109 = (s32[]{:T(128)}, f32[8,64,64]{2,1,0:T(8,128)S(1)}, f32[8,64]{1,0:T(8,128)S(1)}, bf16[2,640,8,64]{1,3,2,0:T(8,128)(2,1)}, bf16[2,640,8,64]{1,3,2,0:T...) while((s32[]{:T(128)}, f32[8,64,64]{2,1,0:T(8,128)S(1)}, ...), condition=%wide.region_19.20_spmd.clone, body=%wide.region_17.19_spmd.sunk.clone | while | flops 3134579200 | bytes 76115248 | solution.py:220
  415.6 7.8 %convolution_convert_fusion.3 = bf16[512,2048]{1,0:T(8,128)(2,1)} fusion(bf16[1280,2048]{1,0:T(8,128)(2,1)} %copy-done.65, f32[1280,512]{0,1:T(8,128)} %copy-done.8, f32[512]{0:T(512)S(1)} %copy-done.51, f32[512]{0:T(512)S(1)} %convert_element_type.365, f32[1280]{0:T(1024)S(1)} %fusion.163, f32[1280]{0:T(1024)S(1)} %broadcast_multiply_fusion), kind=kOutput, calls=%fused_computation.189 | convolution fusion | flops 2688679936 | bytes 9975808 | tf_op jit(solution)/shard_map/nd,nf->df/dot_general | solution.py:351
  423.5 6.8 %convolution_convert_fusion.2 = bf16[2048,512]{1,0:T(8,128)(2,1)} fusion(bf16[1280,2048]{1,0:T(8,128)(2,1)} %get-tuple-element.1120, bf16[1,1,1280,512]{3,2,1,0:T(8,128)(2,1)S(1)} %copy-done.20), kind=kOutput, calls=%fused_computation.188 | convolution fusion | flops 2685403136 | bytes 8650752 | tf_op jit(solution)/shard_map/nf,nd->fd/dot_general | solution.py:343
  433.1 6.3 %fusion.181 = (bf16[512]{0:T(512)(128)(2,1)S(1)}, f32[1280,512]{1,0:T(8,128)}) fusion(bf16[512,1536]{1,0:T(8,128)(2,1)} %all-gather.11.cloned.1.call-done, bf16[1280,512]{1,0:T(8,128)(2,1)} %copy-done.27, bf16[1280,1024]{1,0:T(8,128)(2,1)} %get-tuple-element.1117), kind=kOutput, calls=%fused_computation.258 | convolution fusion | flops 2021785088 | bytes 8127488 | tf_op jit(solution)/shard_map/nf,df->nd/dot_general | solution.py:413
  446.6 22.5 %all-reduce.16 = (bf16[512]{0:T(512)(128)(2,1)S(1)}, bf16[512]{0:T(512)(128)(2,1)S(1)}, bf16[512]{0:T(512)(128)(2,1)S(1)}, bf16[1024]{0:T(1024)(128)(2,1)S(1)}, ...) all-reduce(bf16[512]{0:T(512)(128)(2,1)S(1)} %dynamic-update-slice., ...), channel_id=1, replica_groups=mesh['dp'=8,'seq'=4] {'dp'}, use_global_device_ids=true, to_apply=%add.7 | all-reduce | flops 6656 | bytes 26624
  469.8 10.5 %all-reduce.18 = (bf16[64]{0:T(256)(128)(2,1)S(1)}, bf16[64]{0:T(256)(128)(2,1)S(1)}, bf16[128]{0:T(256)(128)(2,1)S(1)}, bf16[64]{0:T(256)(128)(2,1)S(1)}, bf16[...) all-reduce(bf16[64]{0:T(256)(128)(2,1)S(1)} %dynamic-slice.11, ...), channel_id=1, replica_groups=mesh['dp'=8,'seq'=4] {'seq'}, use_global_device_ids=true, to_apply=%region_23.24 | all-reduce | flops 768 | bytes 3072 | tf_op jit(solution)/shard_map/psum | solution.py:419
  493.1 25.1 %reduce-scatter.9.cloned.1.call-done = bf16[64,2048]{1,0:T(8,128)(2,1)} async-done(((bf16[512,2048]{1,0:T(8,128)(2,1)}), bf16[64,2048]{1,0:T(8,128)(2,1)}) %reduce-scatter.9.cloned.1.call-update) | async-done | bytes 262160 | tf_op jit(solution)/shard_map/reduce_scatter | solution.py:457
  518.2 44.5 %reduce-scatter.11.cloned.1.call-done = bf16[256,512]{1,0:T(8,128)(2,1)} async-done(((bf16[2048,512]{1,0:T(8,128)(2,1)}), bf16[256,512]{1,0:T(8,128)(2,1)}) %reduce-scatter.11.cloned.1.call-update) | async-done | bytes 262160 | tf_op jit(solution)/shard_map/reduce_scatter | solution.py:463
  562.8 6.8 %fusion.136 = bf16[1,1,1280,512]{2,3,1,0:T(8,128)(2,1)S(1)} fusion(f32[1280,512]{0,1:T(8,128)} %copy-done.8, bf16[1280,2048]{1,0:T(8,128)(2,1)} %get-tuple-element.1120, bf16[2048,512]{1,0:T(8,128)(2,1)} %all-gather.15.cloned.1.call-done, f32[512]{0:T(512)S(1)} %convert_element_type.370), kind=kOutput, calls=%fused_computation.192 | convolution fusion | flops 2686320640 | bytes 11274240 | tf_op jit(solution)/shard_map/dot_general | solution.py:337
  571.1 39.1 %all-reduce.22.cloned.1.call-done = (bf16[64,1536]{1,0:T(8,128)(2,1)}, bf16[64,512]{1,0:T(8,128)(2,1)}, bf16[64,2048]{1,0:T(8,128)(2,1)}, bf16[256,512]{1,0:T(8,128)(2,1)}) async-done(((bf16[64,1536]{1,0:T(8,128)(2,1)}, bf16[64,512]{1,0:T(8,128)(2,1)}, bf16[64,2048]{1,0:T(8,128)(2,1)}, bf16[256,512]{1,0:T(8,128)(2,1)}), (bf16[64,1536]{1,0:T(8,128)(2,1)}, bf16[64,512]{1,0:T(8,128)(2,1)}, ...) | async-done | bytes 786448 | tf_op jit(solution)/shard_map/psum | solution.py:421
  (377 shorter events, 264.6 us)
Async XLA Ops:
  7.2 73.6 %all-gather.11.cloned.1.call-start = ((), (), s32[]{:S(2)}) async-start(), calls=%async_computation.4 | async-start | bytes 1769472 | tf_op jit(solution)/shard_map/all_gather | solution.py:249
  7.9 181.3 %all-gather.13.cloned.1.call-start = ((), (), s32[]{:S(2)}) async-start(), calls=%async_computation.5 | async-start | bytes 2359296 | tf_op jit(solution)/shard_map/all_gather | solution.py:257
  8.7 211.0 %all-gather.15.cloned.1.call-start = ((), (), s32[]{:S(2)}) async-start(), calls=%async_computation.6 | async-start | bytes 2359296 | tf_op jit(solution)/shard_map/all_gather | solution.py:259
  9.4 483.7 %reduce-scatter.7.cloned.1.call-start = ((), (), s32[]{:S(2)}) async-start(), calls=%async_computation.8 | async-start | bytes 589824 | tf_op jit(solution)/shard_map/reduce_scatter | solution.py:445
  31.4 49.4 %copy-start.41 = (f32[512]{0:T(512)}, f32[512]{0:T(512)S(1)}, u32[]{:S(2)}) copy-start(f32[512]{0:T(512)S(1)} %convert_element_type.357) | copy-start | bytes 6148
  31.5 49.3 %copy-start.48 = (f32[512]{0:T(512)}, f32[512]{0:T(512)S(1)}, u32[]{:S(2)}) copy-start(f32[512]{0:T(512)S(1)} %convert_element_type.358) | copy-start | bytes 6148
  31.5 38.9 %copy-start.60 = (bf16[256]{0:T(256)(128)(2,1)S(1)}, bf16[256]{0:T(256)(128)(2,1)}, u32[]{:S(2)}) copy-start(bf16[256]{0:T(256)(128)(2,1)} %param.35) | copy-start | bytes 1540
  31.5 47.1 %copy-start.18 = (bf16[1,1,1280,512]{3,2,1,0:T(8,128)(2,1)S(1)}, bf16[1,1,1280,512]{3,2,1,0:T(8,128)(2,1)}, u32[]{:S(2)}) copy-start(bf16[1,1,1280,512]{3,2,1,0:T(8,128)(2,1)} %param.25) | copy-start | bytes 3932164
  33.2 47.6 %copy-start.4 = (bf16[1,1,1280,512]{2,3,1,0:T(8,128)(2,1)}, bf16[1,1,1280,512]{2,3,1,0:T(8,128)(2,1)S(1)}, u32[]{:S(2)}) copy-start(bf16[1,1,1280,512]{2,3,1,0:T(8,128)(2,1)S(1)} %copy.130) | copy-start | bytes 3932164
  33.5 51.2 %copy-start.31 = (f32[1280]{0:T(1024)}, f32[1280]{0:T(1024)S(1)}, u32[]{:S(2)}) copy-start(f32[1280]{0:T(1024)S(1)} %broadcast_multiply_fusion.1) | copy-start | bytes 15364
  33.9 26.0 %copy-start.37 = (f32[1280]{0:T(1024)}, f32[1280]{0:T(1024)S(1)}, u32[]{:S(2)}) copy-start(f32[1280]{0:T(1024)S(1)} %fusion.140) | copy-start | bytes 15364
  33.9 50.8 %copy-start.33 = (f32[1280]{0:T(1024)}, f32[1280]{0:T(1024)S(1)}, u32[]{:S(2)}) copy-start(f32[1280]{0:T(1024)S(1)} %fusion.162) | copy-start | bytes 15364
  70.4 118.9 %copy-start.50 = (f32[512]{0:T(512)}, f32[512]{0:T(512)S(1)}, u32[]{:S(2)}) copy-start(f32[512]{0:T(512)S(1)} %convert_element_type.366) | copy-start | bytes 6148
  189.2 30.4 %copy-start.19 = (bf16[1,1,1280,512]{3,2,1,0:T(8,128)(2,1)S(1)}, bf16[1,1,1280,512]{3,2,1,0:T(8,128)(2,1)}, u32[]{:S(2)}) copy-start(bf16[1,1,1280,512]{3,2,1,0:T(8,128)(2,1)} %param.25) | copy-start | bytes 3932164
  256.0 19.0 %copy-start.26 = (bf16[1280,512]{0,1:T(8,128)(2,1)S(1)}, bf16[1280,512]{0,1:T(8,128)(2,1)}, u32[]{:S(2)}) copy-start(bf16[1280,512]{0,1:T(8,128)(2,1)} %convolution_convert_fusion.1) | copy-start | bytes 3932164
  278.3 21.8 %copy-start.1 = (f32[1,8,64,64]{3,2,1,0:T(8,128)S(1)}, f32[1,8,64,64]{3,2,1,0:T(8,128)}, u32[]{:S(2)}) copy-start(f32[1,8,64,64]{3,2,1,0:T(8,128)} %custom-call.2) | copy-start | bytes 393220
  278.3 21.8 %copy-start.30 = (f32[1,8,64]{2,1,0:T(8,128)S(1)}, f32[1,8,64]{2,1,0:T(8,128)}, u32[]{:S(2)}) copy-start(f32[1,8,64]{2,1,0:T(8,128)} %custom-call.3) | copy-start | bytes 6148
  278.3 21.8 %copy-start.62 = (f32[4]{0:T(128)S(1)}, f32[4]{0:T(128)}, u32[]{:S(2)}) copy-start(f32[4]{0:T(128)} %reverse) | copy-start | bytes 52
  398.1 95.0 %reduce-scatter.5.cloned.1.call-start = ((), (), s32[]{:S(2)}) async-start(), calls=%async_computation.7 | async-start | bytes 1769472 | tf_op jit(solution)/shard_map/reduce_scatter | solution.py:439
  415.5 102.7 %reduce-scatter.9.cloned.1.call-start = ((), (), s32[]{:S(2)}) async-start(), calls=%async_computation.9 | async-start | bytes 2359296 | tf_op jit(solution)/shard_map/reduce_scatter | solution.py:457
  423.5 139.3 %reduce-scatter.11.cloned.1.call-start = ((), (), s32[]{:S(2)}) async-start(), calls=%async_computation.10 | async-start | bytes 2359296 | tf_op jit(solution)/shard_map/reduce_scatter | solution.py:463
  430.3 179.9 %all-reduce.22.cloned.1.call-start = ((), (), s32[]{:S(2)}) async-start(), calls=%async_computation.11 | async-start | bytes 1572864 | tf_op jit(solution)/shard_map/psum | solution.py:421
  445.3 39.2 %copy-start.17 = (bf16[1,1,1280,512]{2,3,1,0:T(8,128)(2,1)S(1)}, bf16[1,1,1280,512]{2,3,1,0:T(8,128)(2,1)}, u32[]{:S(2)}) copy-start(bf16[1,1,1280,512]{2,3,1,0:T(8,128)(2,1)} %copy.142) | copy-start | bytes 3932164
  445.3 39.2 %copy-start.36 = (f32[1280]{0:T(1024)S(1)}, f32[1280]{0:T(1024)}, u32[]{:S(2)}) copy-start(f32[1280]{0:T(1024)} %copy-done.35) | copy-start | bytes 15364
  (53 other events, 202.4 us)
Sparse Core Ops, SparseCore 0:
  9.9 28.5 all-gather.10
  40.4 29.1 all-gather.12
  71.4 28.4 all-gather.14
  398.2 33.0 reduce-scatter.6
  434.8 38.6 reduce-scatter.4
  477.0 41.1 reduce-scatter.8
  521.5 41.2 reduce-scatter.10
  565.6 44.6 all-reduce.21
where the time goes:
time: 635 us; the launch traced here: 624 us
  matrix products  175 us (28%)
  blocking collectives  155 us (24%)
  waiting for transfers between devices  111 us (17%)
  local copies, waits for them, and re-layouts  91.1 us (14%)
  other arithmetic  66.1 us (10%)
  between operations  19.5 us (3%)
    all_gather x4, blocking collectives, entering(): pieces = jax.tree.map(lambda part: lax.all_gather(part, axis), value)  67.7 us
    unnamed x3, blocking collectives  50.5 us
    reduce_scatter x1, waiting for transfers between devices, body(): lax.psum_scatter(summed[10].astype(jnp.bfloat16), 'dp', scatter_dimension...  44.5 us
    psum x1, waiting for transfers between devices, body(): lax.psum(grad_w_qkv.astype(jnp.bfloat16), 'seq').astype(jnp.float32)  39.1 us
    dot_general x1, matrix products, body(): jnp.dot(normed_two_low, weight_up, preferred_element_type=jnp.float32)  30.4 us
    reduce_scatter x1, waiting for transfers between devices, body(): lax.psum_scatter(summed[8].astype(jnp.bfloat16), 'dp', scatter_dimension=...  25.1 us
    unnamed x158, local copies, waits for them, and re-layouts  19.6 us
    convert_element_type x4, local copies, waits for them, and re-layouts, attend_backward(): array.reshape(row_count, head_count * head_size).astype(jnp.bfloat16)  16.1 us
  transfers between devices with their start and end apart: 8, of which 3 were waited for; matrix products, arithmetic and copies ran while one was open for 29% of the time, Pallas kernels for 0%

commit v1 on v0

v1 whole, which is shorter than its diff:
```python
import functools

import jax
import jax.numpy as jnp
from jax import lax
from jax.experimental import pallas as pl
from jax.experimental.pallas import tpu as pltpu
from jax.sharding import PartitionSpec as P

HEADS = 8
CHUNK = 256
TALL = 640
LANES = 128
eps_norm = 1e-05
eps_attn = 1e-06
MESH = pl.DeviceIdType.MESH
f32 = jnp.float32
bf16 = jnp.bfloat16


def dot(a, b, ca, cb):
    return lax.dot_general(a, b, (((ca,), (cb,)), ((), ())), preferred_element_type=f32)


def nn(a, b):
    return dot(a, b, 1, 0)


def nt(a, b):
    return dot(a, b, 1, 1)


def tn(a, b):
    return dot(a, b, 0, 0)


def span(index, size):
    return pl.ds(pl.multiple_of(index * size, size), size)


def lanes_of(shape):
    return lax.broadcasted_iota(jnp.int32, shape, len(shape) - 1)


def rows_of(shape):
    return lax.broadcasted_iota(jnp.int32, shape, len(shape) - 2)


def fold_rows(values):
    rows, width = values.shape
    return jnp.sum(values.reshape(rows // 8, 8, width), axis=0)


def normalised(values):
    width = values.shape[-1]
    mean = jnp.sum(values, axis=-1, keepdims=True) * (1.0 / width)
    centred = values - mean
    variance = jnp.sum(centred * centred, axis=-1, keepdims=True) * (1.0 / width)
    scale = lax.rsqrt(variance + eps_norm)
    return centred * scale, scale


def norm_back(grad, gain, hat, scale):
    width = grad.shape[-1]
    a = grad * gain
    mean_a = jnp.sum(a, axis=-1, keepdims=True) * (1.0 / width)
    mean_ah = jnp.sum(a * hat, axis=-1, keepdims=True) * (1.0 / width)
    return (a - mean_a - hat * mean_ah) * scale


def gelu_pair(x):
    e = jnp.exp(x * x * -0.5)
    z = jnp.abs(x) * 0.7071067811865476
    t = 1.0 / (1.0 + 0.3275911 * z)
    poly = t * (
        0.254829592
        + t * (-0.284496736 + t * (1.421413741 + t * (-1.453152027 + t * 1.061405429)))
    )
    tail = 0.5 * poly * e
    cdf = jnp.where(x >= 0.0, 1.0 - tail, tail)
    return x * cdf, cdf + x * (0.3989422804014327 * e)


class Shape:
    def __init__(self, mesh, rows, width, hidden):
        self.dp = mesh.shape["dp"]
        self.seq = mesh.shape["seq"]
        self.chips = self.dp // 2
        self.side = max(k for k in range(1, self.chips + 1) if k * k <= self.chips and self.chips % k == 0)
        self.rows, self.width, self.hidden = rows, width, hidden
        self.chunks = rows // CHUNK
        self.pairs = width // LANES
        self.sizes = (width, width, 2 * width, width, width, width, hidden, width)
        self.vec_lanes = max(-(-n // self.dp // LANES) * LANES for n in self.sizes)
        w, h, d = width, hidden, self.dp
        self.weights = ((w // d, 3 * w), (w // d, w), (w // d, h), (h // d, w))
        self.gathers = (
            (0, 0, w),
            (0, w, w),
            (0, 2 * w, w),
            (1, 0, w),
            (2, 0, h // 2),
            (2, h // 2, h // 2),
            (3, 0, w),
        )
        self.scatters = (
            (3, 0, w),
            (2, 0, h),
            (1, 0, w),
            (0, 0, w),
            (0, w, w),
            (0, 2 * w, w),
        )


def kernel(
    s,
    lengths,
    x_ref,
    cot_any,
    vec_ref,
    wq_any,
    wo_any,
    wu_any,
    wd_any,
    out_any,
    gin_any,
    gq_out,
    go_out,
    gu_out,
    gd_out,
    vec_out,
    wq,
    wo,
    wu,
    wd,
    cot,
    n1,
    n1t,
    feat,
    acc,
    mask,
    state_in,
    state,
    state_b,
    n2t,
    act,
    hgrad,
    gmid,
    gone,
    vecs,
    vgot,
    vsum,
    vstage,
    vback,
    vz,
    vzback,
    msg,
    msg_in,
    rb0,
    rb1,
    zsrc,
    zr1,
    zr2,
    g_local,
    g_send,
    g_recv,
    v_send,
    v_recv,
    m_send,
    m_recv,
    r_send,
    r_recv,
    io_sem,
):
    dp, seq, chips, side = s.dp, s.seq, s.chips, s.side
    rows, width, hidden = s.rows, s.width, s.hidden
    me, z = lax.axis_index("dp"), lax.axis_index("seq")
    core, chip = lax.rem(me, 2), me // 2
    cy, cx = chip // side, lax.rem(chip, side)
    offsets = [(dy, dx) for dy in range(chips // side) for dx in range(side)][1:]

    def chip_at(dy, dx):
        ny = chips // side
        return lax.rem(cy + dy + ny, ny) * side + lax.rem(cx + dx + side, side)

    heard, dnum, stage_q = n1, cot, hgrad

    sibling = (chip * 2 + 1 - core, z)
    peers = [(chip_at(dy, dx) * 2 + core, z) for dy, dx in offsets]
    z_up, z_down = lax.rem(z + 1, seq), lax.rem(z + seq - 1, seq)

    def remote(src, dst, send, recv, device):
        return pltpu.make_async_remote_copy(
            src_ref=src,
            dst_ref=dst,
            send_sem=send,
            recv_sem=recv,
            device_id=device,
            device_id_type=MESH,
        )

    barrier = pltpu.get_barrier_semaphore()
    for step in range(1, dp):
        pl.semaphore_signal(
            barrier, inc=1, device_id=(lax.rem(me + step, dp), z), device_id_type=MESH
        )
    for step in range(1, seq):
        pl.semaphore_signal(
            barrier, inc=1, device_id=(me, lax.rem(z + step, seq)), device_id_type=MESH
        )
    pl.semaphore_wait(barrier, dp + seq - 2)

    vec_sends = []
    for step in range(1, dp):
        vec_sends.append(
            remote(
                vec_ref,
                vgot.at[me],
                v_send.at[step - 1],
                v_recv.at[step - 1],
                (lax.rem(me + step, dp), z),
            )
        )
        vec_sends[-1].start()
    vgot[me] = vec_ref[...]

    sources = (wq_any, wo_any, wu_any, wd_any)
    weights = (wq, wo, wu, wd)
    parity = lax.rem(z, 2)
    nk = len(peers)

    class Gather:
        def __init__(self, item):
            index, first, columns = s.gathers[item]
            self.buffer, self.source = weights[index], sources[index]
            self.half, self.quarter = columns // 2, columns // 4
            self.mine = first + parity * self.half
            self.other = first + (1 - parity) * self.half
            self.send, self.recv, self.local = g_send.at[item], g_recv.at[item], g_local.at[item]

        def columns(self, first, size):
            return pl.ds(pl.multiple_of(first, LANES), size)

        def part(self, owner, first, size):
            return self.buffer.at[owner // 2, lax.rem(owner, 2), :, self.columns(first, size)]

        def both(self, first, size, which):
            return self.buffer.at[:, which, :, self.columns(first, size)]

        def start(self):
            src = self.source.at[:, self.columns(self.mine, self.half)]
            dst = self.part(me, self.mine, self.half)
            self.own = pltpu.make_async_copy(src, dst, self.local)
            self.own.start()
            self.plane = [
                remote(src, dst, self.send.at[k], self.recv.at[k], peer)
                for k, peer in enumerate(peers)
            ]
            for copy in self.plane:
                copy.start()

        def middle(self):
            self.own.wait()
            for copy in self.plane:
                copy.wait_recv()
            mine, size = self.mine, self.quarter
            self.along = [
                remote(
                    self.both(mine + k * size, size, core),
                    self.both(mine + k * size, size, core),
                    self.send.at[nk + k],
                    self.recv.at[nk + k],
                    (me, (z_up, z_down)[k]),
                )
                for k in range(2)
            ]
            for copy in self.along:
                copy.start()
            self.across = [
                remote(
                    self.both(mine, self.half, core),
                    self.both(mine, self.half, core),
                    self.send.at[nk + 2],
                    self.recv.at[nk + 2],
                    sibling,
                )
            ]
            self.across[0].start()

        def late(self):
            size = self.quarter
            for k in range(2):
                there = self.both(self.other + k * size, size, core)
                remote(there, there, self.send.at[nk + k], self.recv.at[nk + k], sibling).wait_recv()
                copy = remote(there, there, self.send.at[nk + 3 + k], self.recv.at[nk + 3 + k], sibling)
                copy.start()
                self.across.append(copy)

        def finish(self):
            there = self.both(self.mine, self.half, 1 - core)
            remote(there, there, self.send.at[nk + 2], self.recv.at[nk + 2], sibling).wait_recv()
            for k in range(2):
                there = self.both(self.other + k * self.quarter, self.quarter, 1 - core)
                remote(
                    there, there, self.send.at[nk + 3 + k], self.recv.at[nk + 3 + k], sibling
                ).wait_recv()

        def drain(self):
            for copy in self.plane + self.along + self.across:
                copy.wait_send()

    gathers = [Gather(item) for item in range(len(s.gathers))]
    for item in range(3):
        gathers[item].start()
    cot_copy = pltpu.make_async_copy(cot_any, cot, io_sem.at[0])
    cot_copy.start()

    bound_0 = lengths[0]
    bound_1 = bound_0 + lengths[1]
    bound_2 = bound_1 + lengths[2]
    first_row = z * rows

    def segment(position):
        return sum((position >= bound).astype(jnp.int32) for bound in (bound_0, bound_1, bound_2))

    def same(a, b):
        return (a == b).astype(f32)

    prior = jnp.where(first_row > 0, segment(first_row - 1), -1)
    last = segment(first_row + rows - 1)

    def before(c):
        return jnp.where(first_row + c * CHUNK > 0, segment(first_row + c * CHUNK - 1), -1)

    def ending(c):
        return segment(first_row + (c + 1) * CHUNK - 1)

    def in_segment(c, which):
        shape = (CHUNK, LANES)
        return (segment(first_row + c * CHUNK + rows_of(shape)) == which).astype(f32)

    square = (CHUNK, CHUNK)
    pair = (LANES, LANES)
    lane_low = lanes_of((CHUNK, LANES)) < 64
    block_diag = (
        (lanes_of((LANES, 2 * LANES)) // 64) % 2 == rows_of((LANES, 2 * LANES)) // 64
    ).astype(f32)
    low_pair = lanes_of(pair) < 64
    low_half = (lanes_of(pair) & 63) < 32
    ones_low = lane_low.astype(bf16)
    ones_high = 1.0 - ones_low

    def mask_body(c, carry):
        down, across = rows_of(square), lanes_of(square)
        base = first_row + c * CHUNK
        alike = segment(base + down) == segment(base + across)
        mask[c] = (alike & (across <= down)).astype(f32).astype(bf16)
        return carry

    lax.fori_loop(0, s.chunks, mask_body, 0)

    for step in range(1, dp):
        source = lax.rem(me - step + dp, dp)
        remote(
            vec_ref, vgot.at[source], v_send.at[step - 1], v_recv.at[step - 1], (source, z)
        ).wait_recv()

    def one_hot(n):
        piece = n // dp
        tall = -(-piece // LANES) * LANES
        shape = (tall, n)
        return ((lanes_of(shape) & (piece - 1)) == rows_of(shape)).astype(f32).astype(bf16)

    def owner_mask(n):
        piece = n // dp
        shape = (dp, n)
        low = rows_of(shape) * piece
        return (lanes_of(shape) >= low) & (lanes_of(shape) < low + piece)

    for k, n in enumerate(s.sizes):
        table = one_hot(n)
        pieces = vgot[:, k, : table.shape[0]].astype(bf16)
        spread = jnp.where(owner_mask(n), nn(pieces, table), 0.0)
        vecs[k : k + 1, :n] = jnp.sum(spread, axis=0, keepdims=True)

    starts = [sum(s.sizes[:k]) for k in range(len(s.sizes))]

    def collect(k, first, values):
        at = starts[k] + first
        vsum[:, at : at + values.shape[1]] += fold_rows(values)

    gain_one, shift_one = vecs[0:1, :width], vecs[1:2, :width]
    for k, n in enumerate(s.sizes):
        vsum[:, starts[k] : starts[k] + n] = jnp.zeros((8, n), f32)

    def norm_body(c, carry):
        here = span(c, CHUNK)
        hat, _ = normalised(x_ref[here, :].astype(f32))
        normed = (hat * gain_one + shift_one).astype(bf16)
        n1[here, :] = normed
        n1t[:, here] = normed.T
        return carry

    lax.fori_loop(0, s.chunks, norm_body, 0)

    for item in range(3):
        gathers[item].middle()
    for item in range(3, len(gathers)):
        gathers[item].start()
    for item in range(3):
        gathers[item].late()
    for item in range(3):
        gathers[item].finish()
        weight = wq[:, :, :, item * width : (item + 1) * width].reshape(width, width)
        if item < 2:
            bias = vecs[2:3, item * width : (item + 1) * width]

        def project_body(c, carry):
            here = span(c, TALL)
            mixed = nn(n1[here, :], weight)
            if item < 2:
                mixed = mixed + bias
                mixed = jnp.where(mixed > 0.0, mixed + 1.0, jnp.exp(jnp.minimum(mixed, 0.0)))
            feat[here, item * width : (item + 1) * width] = mixed.astype(bf16)
            return carry

        lax.fori_loop(0, rows // TALL, project_body, 0)

    def cut(here, part, p):
        first = part * width + p * LANES
        return feat[here, first : first + LANES]

    for p in range(s.pairs):
        state[p] = jnp.zeros((LANES, 2 * LANES), f32)

    def state_body(c, carry):
        here = span(c, CHUNK)
        keep = same(ending(c), before(c))
        chosen = in_segment(c, ending(c)).astype(bf16)
        for p in range(s.pairs):
            wide = jnp.concatenate([cut(here, 2, p) * chosen, chosen], axis=1)
            now = state[p]
            state_in[c, p] = now
            state[p] = keep * now + tn(cut(here, 1, p), wide) * block_diag
        return carry

    lax.fori_loop(0, s.chunks, state_body, 0)

    def spread_ends(right):
        return 0.5 * (right + pltpu.roll(right, 32, 1))

    def packed(slot):
        halves = []
        ends = []
        for p in range(s.pairs):
            left = state[p, :, :LANES]
            right = state[p, :, LANES:]
            halves.append(left + pltpu.roll(left, 64, 1))
            ends.append(spread_ends(right + pltpu.roll(right, 64, 1)))
        for q in range(s.pairs // 2):
            msg[slot, q] = jnp.where(low_pair, halves[2 * q], halves[2 * q + 1]).astype(bf16)
        total = ends[0]
        lanes = LANES // s.pairs
        for p in range(1, s.pairs):
            total = jnp.where(lanes_of(pair) // lanes == p, ends[p], total)
        upper = total.astype(bf16).astype(f32)
        total = jnp.where(lanes_of(pair) % lanes < lanes // 2, upper, total - upper)
        msg[slot, s.pairs // 2] = total.astype(bf16)

    def unpacked(slot, step, p):
        sums = msg_in[slot, step, p // 2].astype(f32)
        turned = pltpu.roll(sums, 64, 1)
        left = jnp.where(low_pair, sums, turned) if p % 2 == 0 else jnp.where(low_pair, turned, sums)
        first = p * (LANES // s.pairs)
        middle = first + LANES // s.pairs // 2
        ends = msg_in[slot, step, s.pairs // 2].astype(f32)
        right = ends[:, first : first + 1] + ends[:, middle : middle + 1]
        return jnp.concatenate([left, jnp.broadcast_to(right, pair)], axis=1) * block_diag

    def message(slot, step, forward):
        target = lax.rem(z + step, seq) if forward else lax.rem(z - step + seq, seq)
        return remote(
            msg.at[slot],
            msg_in.at[slot, step - 1],
            m_send.at[slot, step - 1],
            m_recv.at[slot, step - 1],
            (me, target),
        )

    def send_states(slot, forward):
        packed(slot)
        for step in range(1, seq):

            @pl.when((z + step < seq) if forward else (z - step >= 0))
            def _():
                message(slot, step, forward).start()

    def take_states(slot, forward):
        for p in range(s.pairs):
            state[p] = jnp.zeros((LANES, 2 * LANES), f32)
        for step in range(1, seq):

            @pl.when((z - step >= 0) if forward else (z + step < seq))
            def _():
                message(slot, step, forward).wait_recv()
                if forward:
                    weight = same(segment((z - step + 1) * rows - 1), prior)
                else:
                    weight = same(segment((z + step) * rows - 1), last)
                for p in range(s.pairs):
                    state[p] = state[p] + weight * unpacked(slot, step - 1, p)

    def drain_states(slot, forward):
        for step in range(1, seq):

            @pl.when((z + step < seq) if forward else (z - step >= 0))
            def _():
                message(slot, step, forward).wait_send()

    send_states(0, True)
    gathers[3].middle()

    def inside_body(c, carry):
        here = span(c, CHUNK)
        seen = mask[c]
        for p in range(s.pairs):
            q, k, v = cut(here, 0, p), cut(here, 1, p), cut(here, 2, p)
            k_low, v_low = k * ones_low, v * ones_low
            k_high, v_high = k * ones_high, v * ones_high
            s_low = nt(q, k_low).astype(bf16) * seen
            s_high = nt(q, k_high).astype(bf16) * seen
            acc[here, 2 * p * LANES : (2 * p + 2) * LANES] = nn(
                s_low, jnp.concatenate([v_low, ones_low], axis=1)
            ) + nn(s_high, jnp.concatenate([v_high, ones_high], axis=1))
        return carry

    lax.fori_loop(0, s.chunks, inside_body, 0)
    gathers[3].late()
    for item in range(4, len(gathers)):
        gathers[item].middle()
    take_states(0, True)

    def join_body(c, carry):
        here = span(c, CHUNK)
        live = in_segment(c, before(c))
        carried = same(before(c), prior)
        for p in range(s.pairs):
            whole = state_in[c, p] + carried * state[p]
            upper = whole.astype(bf16)
            lower = (whole - upper.astype(f32)).astype(bf16)
            state_b[c, p, :LANES] = upper
            state_b[c, p, LANES:] = lower
            q = cut(here, 0, p)
            extra = nn(jnp.concatenate([q, q], axis=1), state_b[c, p])
            first = 2 * p * LANES
            numerator = acc[here, first : first + LANES] + live * extra[:, :LANES]
            denominator = acc[here, first + LANES : first + 2 * LANES] + live * extra[:, LANES:]
            inverse = 1.0 / (denominator + eps_attn)
            result = numerator * inverse
            acc[here, first : first + LANES] = result
            acc[here, first + LANES : first + 2 * LANES] = inverse
            heard[here, p * LANES : (p + 1) * LANES] = result.astype(bf16)
        return carry

    lax.fori_loop(0, s.chunks, join_body, 0)
    gathers[3].finish()
    for item in range(4, len(gathers)):
        gathers[item].late()
    for item in range(4, len(gathers)):
        gathers[item].finish()
    cot_copy.wait()

    bias_out, gain_two, shift_two = (vecs[k : k + 1, :width] for k in (3, 4, 5))
    bias_down = vecs[7:8, :width]
    tile = 512
    tall = s.weights[0][0]

    def forward_body(c, carry):
        here = span(c, TALL)
        middle = (
            x_ref[here, :].astype(f32)
            + nn(heard[here, :], wo[...].reshape(width, width))
            + bias_out
        )
        hat, scale = normalised(middle)
        normed = (hat * gain_two + shift_two).astype(bf16)
        n2t[:, here] = normed.T
        branch = cot[here, :]
        collect(7, 0, branch.astype(f32))
        total = middle + bias_down
        back = jnp.zeros((TALL, width), f32)
        for t in range(hidden // tile):
            cols = slice(t * tile, (t + 1) * tile)
            up = wu[:, :, :, cols].reshape(width, tile)
            per = chips * tile // hidden
            down = wd[t * per : (t + 1) * per].reshape(tile, width)
            active, slope = gelu_pair(nn(normed, up) + vecs[6:7, cols])
            active = active.astype(bf16)
            act[here, cols] = active
            grad = (slope * nt(branch, down)).astype(bf16)
            hgrad[span(c, TALL // (2 * tall)), :, :, cols] = grad.reshape(TALL // (2 * tall), 2, tall, tile)
            collect(6, t * tile, grad.astype(f32))
            total = total + nn(active, down)
            back = back + nt(grad, up)
        out_any_rows = total.astype(bf16)
        gone[here, :] = out_any_rows
        copy = pltpu.make_async_copy(gone.at[here, :], out_any.at[here, :], io_sem.at[1])
        copy.start()
        collect(4, 0, back * hat)
        collect(5, 0, back)
        grad_middle = branch.astype(f32) + norm_back(back, gain_two, hat, scale)
        gmid[here, :] = grad_middle
        copy.wait()
        low = grad_middle.astype(bf16)
        gone[here, :] = low
        collect(3, 0, low.astype(f32))
        return carry

    lax.fori_loop(0, rows // TALL, forward_body, 0)
    for gather in gathers:
        gather.drain()

    stages = (stage_q, wo, wu, wd)
    results = (gq_out, go_out, gu_out, gd_out)

    class Scatter:
        def __init__(self, item):
            index, first, columns = s.scatters[item]
            self.stage, self.result = stages[index], results[index]
            self.first, self.count, self.height = first, columns, s.weights[index][0]
            self.cols = pl.ds(first, columns)
            shared = item - len(s.scatters) + 3
            if shared >= 0:
                here = pl.ds(shared * self.height, self.height)
                self.rb0, self.rb1 = rb0[0].at[:, here], rb1[0].at[:, here]
            else:
                self.rb0, self.rb1 = rb0[item], rb1[item]
            self.zsrc, self.zr1, self.zr2 = zsrc[item], zr1[item], zr2[item]
            self.send, self.recv = r_send.at[item], r_recv.at[item]

        def start(self):
            self.across = remote(
                self.stage.at[pl.ds(0, chips), 1 - core, :, self.cols],
                self.rb0,
                self.send.at[0],
                self.recv.at[0],
                sibling,
            )
            self.across.start()

        def plane(self):
            self.across.wait_recv()

            def add(k, carry):
                here = (k, core, slice(None), self.cols)
                self.stage[here] = (
                    self.stage[here].astype(f32) + self.rb0[k].astype(f32)
                ).astype(bf16)
                return carry

            lax.fori_loop(0, chips, add, 0)
            self.sends = [
                remote(
                    self.stage.at[peer[0] // 2, core, :, self.cols],
                    self.rb1.at[k],
                    self.send.at[1 + k],
                    self.recv.at[1 + k],
                    peer,
                )
                for k, peer in enumerate(peers)
            ]
            for copy in self.sends:
                copy.start()

        def exchange(self, source, target, base, swap):
            half = self.count // 2
            partners = (z + 1 - 2 * parity, seq - 1 - z)
            copies = [
                remote(
                    source.at[:, k * half : (k + 1) * half],
                    target.at[:, k * half : (k + 1) * half],
                    self.send.at[base + k],
                    self.recv.at[base + k],
                    (me, partners[1 - k if swap else k]),
                )
                for k in range(2)
            ]
            for copy in copies:
                copy.start()
            return copies

        def along(self):
            for copy in self.sends:
                copy.wait_recv()
            total = self.stage[chip, core, :, self.cols].astype(f32)
            for k in range(nk):
                total = total + self.rb1[k].astype(f32)
            self.zsrc[...] = total.astype(bf16)
            self.first_pair = self.exchange(self.zsrc, self.zr1, nk + 1, False)

        def along_again(self):
            for copy in self.first_pair:
                copy.wait()
            self.zsrc[...] = (self.zsrc[...].astype(f32) + self.zr1[...].astype(f32)).astype(bf16)
            self.second_pair = self.exchange(self.zsrc, self.zr2, nk + 3, True)

        def finish(self):
            for copy in self.second_pair:
                copy.wait_recv()
            self.result[:, self.cols] = (
                self.zsrc[...].astype(f32) + self.zr2[...].astype(f32)
            ).astype(bf16)

        def drain(self):
            self.across.wait_send()
            for copy in self.sends + self.second_pair:
                copy.wait_send()

    scatters = [Scatter(item) for item in range(len(s.scatters))]
    down_item, up_item, out_item = scatters[:3]
    qkv_items = scatters[3:]

    def down_body(c, carry):
        per = chips * tile // hidden
        grad = tn(act[:, span(c, tile)], cot[...]).astype(bf16)
        wd[pl.ds(c * per, per)] = grad.reshape(per, 2, hidden // dp, width)
        return carry

    lax.fori_loop(0, hidden // tile, down_body, 0)
    down_item.start()

    bd_square = block_diag[:, :LANES].astype(bf16)
    head_sum = jnp.concatenate([bd_square, bd_square], axis=0)
    lane_hi = (lanes_of((CHUNK, LANES)) & 63) < 32

    def heads_body(c, carry):
        here = span(c, CHUNK)
        back = nt(gone[here, :], wo[...].reshape(width, width)).astype(bf16).astype(f32)
        for p in range(s.pairs):
            first = 2 * p * LANES
            result = acc[here, first : first + LANES]
            inverse = acc[here, first + LANES : first + 2 * LANES]
            grad = back[:, p * LANES : (p + 1) * LANES]
            dnum[here, p * LANES : (p + 1) * LANES] = (grad * inverse).astype(bf16)
            product = grad * result
            upper = product.astype(bf16)
            lower = (product - upper.astype(f32)).astype(bf16)
            total = nn(jnp.concatenate([upper, lower], axis=1), head_sum)
            value = total * inverse * (-1.0 / 32.0)
            upper = value.astype(bf16)
            lower = value - upper.astype(f32)
            act[here, 3 * width + p * LANES : 3 * width + (p + 1) * LANES] = jnp.where(
                lane_hi, upper.astype(f32), lower
            ).astype(bf16)
        return carry

    lax.fori_loop(0, s.chunks, heads_body, 0)

    def grads_of(here, p):
        first = 3 * width + p * LANES
        return dnum[here, p * LANES : (p + 1) * LANES], act[here, first : first + LANES]

    for p in range(s.pairs):
        state[p] = jnp.zeros((LANES, 2 * LANES), f32)

    def gstate_body(step, carry):
        c = s.chunks - 1 - step
        here = span(c, CHUNK)
        keep = same(ending(c), before(c))
        live = in_segment(c, before(c)).astype(bf16)
        for p in range(s.pairs):
            now = state[p]
            state_in[c, p] = now
            wide = jnp.concatenate(grads_of(here, p), axis=1)
            state[p] = keep * now + tn(cut(here, 0, p) * live, wide) * block_diag
        return carry

    lax.fori_loop(0, s.chunks, gstate_body, 0)
    send_states(1, False)
    down_item.plane()

    def up_body(c, carry):
        cols = span(c, tile)
        grad = nn(n2t[...], hgrad[:, :, :, cols].reshape(rows, tile)).astype(bf16)
        wu[:, :, :, cols] = grad.reshape(chips, 2, width // dp, tile)
        return carry

    lax.fori_loop(0, hidden // tile, up_body, 0)
    up_item.start()
    wo[...] = tn(heard[...], gone[...]).astype(bf16).reshape(chips, 2, width // dp, width)
    out_item.start()
    down_item.along()
    up_item.plane()
    out_item.plane()
    down_item.along_again()
    take_states(1, False)

    def back_body(c, carry):
        here = span(c, CHUNK)
        seen = mask[c]
        seen_t = seen.T
        live = in_segment(c, before(c))
        chosen = in_segment(c, ending(c))
        carried = same(ending(c), last)
        for p in range(s.pairs):
            q, k, v = cut(here, 0, p), cut(here, 1, p), cut(here, 2, p)
            dn, dd = grads_of(here, p)
            wide = jnp.concatenate([dn, dd], axis=1)
            k_low, k_high = k * ones_low, k * ones_high
            v_low = jnp.concatenate([v * ones_low, ones_low], axis=1)
            v_high = jnp.concatenate([v * ones_high, ones_high], axis=1)
            q_low, q_high = q * ones_low, q * ones_high
            dn_low, dn_high = dn * ones_low, dn * ones_high
            ahead = state_in[c, p] + carried * state[p]
            sums = ahead[:, LANES:]
            sums = 2.0 * spread_ends(sums + pltpu.roll(sums, 64, 1)) * block_diag[:, LANES:]
            upper = sums.astype(bf16).astype(f32)
            sums = jnp.where(low_half, upper, sums - upper)
            ahead = jnp.concatenate([ahead[:, :LANES], sums], axis=1).astype(bf16)
            ds_low = nt(wide, v_low).astype(bf16) * seen
            ds_high = nt(wide, v_high).astype(bf16) * seen
            gq = nn(ds_low, k_low) + nn(ds_high, k_high) + live * (
                nt(wide, state_b[c, p, :LANES]) + nt(wide, state_b[c, p, LANES:])
            )
            dst_low = nt(v_low, wide).astype(bf16) * seen_t
            dst_high = nt(v_high, wide).astype(bf16) * seen_t
            v_ones = jnp.concatenate([v, jnp.ones_like(v)], axis=1)
            gk = nn(dst_low, q_low) + nn(dst_high, q_high) + chosen * nt(v_ones, ahead)
            st_low = nt(k_low, q).astype(bf16) * seen_t
            st_high = nt(k_high, q).astype(bf16) * seen_t
            gv = nn(st_low, dn_low) + nn(st_high, dn_high) + chosen * nn(k, ahead[:, :LANES])
            for part, grad in ((0, gq), (1, gk), (2, gv)):
                grad = grad.astype(bf16)
                first = part * width + p * LANES
                if part < 2:
                    slope = jnp.minimum((q, k)[part].astype(f32), 1.0)
                    grad = (grad.astype(f32) * slope).astype(bf16)
                    collect(2, first, grad.astype(f32))
                act[here, first : first + LANES] = grad
        return carry

    lax.fori_loop(0, s.chunks, back_body, 0)
    down_item.finish()
    up_item.along()
    out_item.along()

    for part in range(3):
        cols = slice(part * width, (part + 1) * width)
        grad = nn(n1t[...], act[:, cols]).astype(bf16)
        stage_q[:chips, :, :, cols] = grad.reshape(chips, 2, width // dp, width)
        qkv_items[part].start()
    up_item.along_again()
    out_item.along_again()
    for item in qkv_items:
        item.plane()

    def input_body(c, carry):
        here = span(c, TALL)
        grad = nt(act[here, : 3 * width], wq[...].reshape(width, 3 * width))
        hat, scale = normalised(x_ref[here, :].astype(f32))
        collect(0, 0, grad * hat)
        collect(1, 0, grad)
        gmid[here, :] = gmid[here, :] + norm_back(grad, gain_one, hat, scale)
        pltpu.make_async_copy(gmid.at[here, :], gin_any.at[here, :], io_sem.at[2 + c]).start()
        return carry

    lax.fori_loop(0, rows // TALL, input_body, 0)

    for k, n in enumerate(s.sizes):
        table = one_hot(n)
        row = jnp.sum(vsum[:, starts[k] : starts[k] + n], axis=0, keepdims=True)
        spread = jnp.where(owner_mask(n), jnp.broadcast_to(row, (dp, n)), 0.0).astype(bf16)
        pieces = nt(spread, table)
        if pieces.shape[1] < s.vec_lanes:
            pad = jnp.zeros((dp, s.vec_lanes - pieces.shape[1]), f32)
            pieces = jnp.concatenate([pieces, pad], axis=1)
        vstage[:, k, :] = pieces
    vec_back = []
    for step in range(1, dp):
        target = lax.rem(me + step, dp)
        vec_back.append(
            remote(
                vstage.at[target],
                vback.at[step - 1],
                v_send.at[dp - 2 + step],
                v_recv.at[dp - 2 + step],
                (target, z),
            )
        )
        vec_back[-1].start()
    up_item.finish()
    out_item.finish()
    for item in qkv_items:
        item.along()
    for copy in vec_back:
        copy.wait_recv()
    total = vstage[me]
    for step in range(dp - 1):
        total = total + vback[step]
    vz[...] = total
    vec_z = []
    for step in range(1, seq):
        vec_z.append(
            remote(
                vz,
                vzback.at[step - 1],
                v_send.at[2 * dp - 3 + step],
                v_recv.at[2 * dp - 3 + step],
                (me, lax.rem(z + step, seq)),
            )
        )
        vec_z[-1].start()
    for item in qkv_items:
        item.along_again()
    for copy in vec_z:
        copy.wait_recv()
    terms = [vz[...]] + [vzback[step] for step in range(seq - 1)]
    while len(terms) > 1:
        half = len(terms) // 2
        terms = [terms[i] + terms[i + half] for i in range(half)]
    vec_out[...] = terms[0]
    for item in qkv_items:
        item.finish()

    for c in range(rows // TALL):
        here = pl.ds(c * TALL, TALL)
        pltpu.make_async_copy(gmid.at[here, :], gin_any.at[here, :], io_sem.at[2 + c]).wait()
    drain_states(0, True)
    drain_states(1, False)
    for copy in vec_sends + vec_back + vec_z:
        copy.wait_send()
    for item in scatters:
        item.drain()


def solution(mesh):
    def body(inputs, lengths, cotangent, *params):
        gain_one, shift_one, w_qkv, b_qk, w_out, b_out, gain_two, shift_two, w_up, b_up, w_down, b_down = params
        packs, rows, width = inputs.shape[1:]
        hidden = w_up.shape[1]
        s = Shape(mesh, rows, width, hidden)
        dp, seq, chips, pairs = s.dp, s.seq, s.chips, s.pairs
        nk = chips - 1
        vectors = (gain_one, shift_one, b_qk, b_out, gain_two, shift_two, b_up, b_down)
        vec = jnp.stack(
            [jnp.pad(v.astype(f32), (0, s.vec_lanes - v.shape[0])) for v in vectors]
        )
        vmem = pl.BlockSpec(memory_space=pltpu.VMEM)
        anywhere = pl.BlockSpec(memory_space=pl.ANY)
        grids = [(chips, 2) + shape for shape in s.weights]
        shapes = [(s.weights[index][0], columns) for index, _, columns in s.scatters]
        dma = pltpu.SemaphoreType.DMA
        tall = s.weights[0][0]
        scratch = (
            [pltpu.VMEM(grid, bf16) for grid in grids]
            + [
                pltpu.VMEM((rows, width), bf16),
                pltpu.VMEM((rows, width), bf16),
                pltpu.VMEM((width, rows), bf16),
                pltpu.VMEM((rows, 3 * width), bf16),
                pltpu.VMEM((rows, 2 * width), f32),
                pltpu.VMEM((s.chunks, CHUNK, CHUNK), bf16),
                pltpu.VMEM((s.chunks, pairs, LANES, 2 * LANES), f32),
                pltpu.VMEM((pairs, LANES, 2 * LANES), f32),
                pltpu.VMEM((s.chunks, pairs, 2 * LANES, 2 * LANES), bf16),
                pltpu.VMEM((width, rows), bf16),
                pltpu.VMEM((rows, hidden), bf16),
                pltpu.VMEM((rows // (2 * tall), 2, tall, hidden), bf16),
                pltpu.VMEM((rows, width), f32),
                pltpu.VMEM((rows, width), bf16),
                pltpu.VMEM((8, hidden), f32),
                pltpu.VMEM((dp, 8, s.vec_lanes), f32),
                pltpu.VMEM((8, sum(s.sizes)), f32),
                pltpu.VMEM((dp, 8, s.vec_lanes), f32),
                pltpu.VMEM((dp - 1, 8, s.vec_lanes), f32),
                pltpu.VMEM((8, s.vec_lanes), f32),
                pltpu.VMEM((seq - 1, 8, s.vec_lanes), f32),
                pltpu.VMEM((2, pairs // 2 + 1, LANES, LANES), bf16),
                pltpu.VMEM((2, seq - 1, pairs // 2 + 1, LANES, LANES), bf16),
                [pltpu.VMEM((chips,) + shape, bf16) for shape in shapes[:3]],
                [pltpu.VMEM((nk,) + shape, bf16) for shape in shapes[:3]],
                [pltpu.VMEM(shape, bf16) for shape in shapes],
                [pltpu.VMEM(shape, bf16) for shape in shapes],
                [pltpu.VMEM(shape, bf16) for shape in shapes],
                dma((len(s.gathers),)),
                dma((len(s.gathers), nk + 5)),
                dma((len(s.gathers), nk + 5)),
                dma((2 * dp - 2 + seq - 1,)),
                dma((2 * dp - 2 + seq - 1,)),
                dma((2, seq - 1)),
                dma((2, seq - 1)),
                dma((len(s.scatters), nk + 5)),
                dma((len(s.scatters), nk + 5)),
                dma((2 + rows // TALL,)),
            ]
        )
        outs = pl.pallas_call(
            functools.partial(kernel, s),
            out_shape=(
                jax.ShapeDtypeStruct((rows, width), bf16),
                jax.ShapeDtypeStruct((rows, width), f32),
            )
            + tuple(jax.ShapeDtypeStruct(shape, bf16) for shape in s.weights)
            + (jax.ShapeDtypeStruct((8, s.vec_lanes), f32),),
            in_specs=[pl.BlockSpec(memory_space=pltpu.SMEM), vmem, anywhere, vmem]
            + [anywhere] * 4,
            out_specs=(anywhere, anywhere) + (vmem,) * 5,
            scratch_shapes=scratch,
            compiler_params=pltpu.CompilerParams(
                collective_id=0, has_side_effects=True, vmem_limit_bytes=63 << 20
            ),
            name="layer",
        )(
            lengths.reshape(3),
            inputs.reshape(rows, width),
            cotangent.reshape(rows, width),
            vec,
            w_qkv,
            w_out,
            w_up,
            w_down,
        )
        out, gin, g_qkv, g_out, g_up, g_down, g_vec = outs
        pieces = [g_vec[k, : v.shape[0]] for k, v in enumerate(vectors)]
        return (
            out.reshape(inputs.shape),
            gin.reshape(inputs.shape),
            pieces[0],
            pieces[1],
            g_qkv.astype(f32),
            pieces[2],
            g_out.astype(f32),
            pieces[3],
            pieces[4],
            pieces[5],
            g_up.astype(f32),
            pieces[6],
            g_down.astype(f32),
            pieces[7],
        )

    rows_spec = P("dp", None, "seq", None)
    one, two = P("dp"), P("dp", None)
    params = (one, one, two, one, two, one, one, one, two, one, two, one)
    return jax.shard_map(
        body,
        mesh=mesh,
        in_specs=(rows_spec, P("dp", None, None), rows_spec) + params,
        out_specs=(rows_spec, rows_spec) + params,
        check_vma=False,
    )
```

time: 635 us -> 185 us (0.29); the launches traced: 624 us -> 185 us
  matrix products: 175 us -> 0 us
  Pallas kernels: 0 us -> 166 us
  blocking collectives: 155 us -> 0 us
  waiting for transfers between devices: 111 us -> 0 us
  local copies, waits for them, and re-layouts: 91.1 us -> 12.9 us
  other arithmetic: 66.1 us -> 5.62 us
  between operations: 19.5 us -> 0.69 us
    dot_general x46 -> x0, matrix products: 175 us -> none  [the longest x1 30.4 us: body(): jnp.dot(normed_two_low, weight_up, preferred_element_type=jnp.float32)]
    pallas_call x0 -> x1, Pallas kernels: none -> 166 us  [body(): pl.pallas_call(functools.partial(kernel, s), out_shape=(jax.ShapeDtypeStr...]
    all_gather x7 -> x0, blocking collectives: 94.1 us -> none  [the longest x4 67.7 us: entering(): pieces = jax.tree.map(lambda part: lax.all_gather(part, axis), value)]
    reduce_scatter x4 -> x0, waiting for transfers between devices: 69.7 us -> none  [the longest x1 44.5 us: body(): lax.psum_scatter(summed[10].astype(jnp.bfloat16), 'dp', scatter_dimension...]
    unnamed x3 -> x0, blocking collectives: 50.5 us -> none
    psum x1 -> x0, waiting for transfers between devices: 39.1 us -> none  [body(): lax.psum(grad_w_qkv.astype(jnp.bfloat16), 'seq').astype(jnp.float32)]
    convert_element_type x8 -> x0, local copies, waits for them, and re-layouts: 27.2 us -> none  [the longest x4 16.1 us: attend_backward(): array.reshape(row_count, head_count * head_size).astype(jnp.bfloat16)]
    reduce_sum x15 -> x0, other arithmetic: 21.9 us -> none  [the longest x3 7.58 us: norm_layer(): return centred * lax.rsqrt(variance + eps_norm) * scale_gain + scale_shift]
  transfers between devices with their start and end apart: 8 -> 0, of which waited for: 3 -> 0; matrix products, arithmetic and copies ran while one was open for 29% -> 0% of each run, Pallas kernels for 0% -> 0%
where the time goes in v1:
time: 185 us
  Pallas kernels  166 us (90%)
  local copies, waits for them, and re-layouts  12.9 us (7%)
  other arithmetic  5.62 us (3%)
    pallas_call x1, Pallas kernels, body(): pl.pallas_call(functools.partial(kernel, s), out_shape=(jax.ShapeDtypeStr...  166 us
    pad x7, local copies, waits for them, and re-layouts, body(): jnp.pad(v.astype(f32), (0, s.vec_lanes - v.shape[0]))  4.62 us
    unnamed x10, local copies, waits for them, and re-layouts  3.72 us

profile of v1, /device:TPU:0, one launch (start us, length us, event | category | flops | bytes accessed | tf_op | source)
XLA Modules:
  0.0 184.9 jit_solution(8215427022813585153)
XLA Ops:
  0.6 0.7 pad.30
  1.3 0.7 pad.31
  2.0 0.7 pad.32
  2.6 0.7 pad.33
  3.3 0.7 pad.34
  4.0 0.7 pad.35
  4.7 0.7 pad.36
  5.3 0.7 stack.43
  6.0 0.6 stack.46.vec_ref
  6.6 165.6 %layer.1 = (bf16[1280,512]{1,0:T(8,128)(2,1)}, f32[1280,512]{1,0:T(8,128)}, bf16[64,1536]{1,0:T(8,128)(2,1)}, bf16[64,512]{1,0:T(8,128)(2,1)}, bf16[64,2048]{1,0...) custom-call(s32[3]{0:T(128)} %bitcast.25, bf16[1280,512]{1,0:T(8,128)(2,1)} %bitcast.21, ...), custom_call_target="tpu_custom_call" | custom-call | tf_op jit(solution)/shard_map/layer/pallas_call | solution.py:998
  172.3 0.0 copy-start.2
  172.3 0.0 copy-start.3
  172.3 0.0 copy-start.1
  172.3 1.4 slice_bitcast_fusion
  173.7 1.3 slice.30
  175.0 1.2 slice_bitcast_fusion.4
  176.2 1.8 convert_element_type.31
  177.9 1.8 convert_element_type.32
  179.7 0.8 convert_element_type.29
  180.5 0.0 copy-done.3
  180.5 0.7 convert_element_type.30
  181.2 1.1 copy.31
  182.2 1.2 copy-done
  183.4 1.5 copy.32
  (11 shorter events, 0.1 us)
Async XLA Ops:
  172.3 7.5 %copy-start.2 = (bf16[64,1536]{1,0:T(8,128)(2,1)S(1)}, bf16[64,1536]{1,0:T(8,128)(2,1)}, u32[]{:S(2)}) copy-start(bf16[64,1536]{1,0:T(8,128)(2,1)} %get-tuple-element.24) | copy-start | bytes 589828
  172.3 8.3 %copy-start.3 = (bf16[64,512]{1,0:T(8,128)(2,1)S(1)}, bf16[64,512]{1,0:T(8,128)(2,1)}, u32[]{:S(2)}) copy-start(bf16[64,512]{1,0:T(8,128)(2,1)} %get-tuple-element.25) | copy-start | bytes 196612
  172.3 8.9 %copy-start.1 = (bf16[1280,512]{1,0:T(8,128)(2,1)S(1)}, bf16[1280,512]{1,0:T(8,128)(2,1)}, u32[]{:S(2)}) copy-start(bf16[1280,512]{1,0:T(8,128)(2,1)} %get-tuple-element.21) | copy-start | bytes 3932164
  181.2 2.2 %copy-start = (f32[1280,512]{1,0:T(8,128)S(1)}, f32[1280,512]{1,0:T(8,128)}, u32[]{:S(2)}) copy-start(f32[1280,512]{1,0:T(8,128)} %get-tuple-element.22) | copy-start | bytes 7864324

commit v2 on v1

--- a/solution.py
+++ b/solution.py
@@ -98,11 +98,9 @@
             (0, 0, w),
             (0, w, w),
             (0, 2 * w, w),
+            (3, 0, w),
             (1, 0, w),
-            (2, 0, h // 2),
-            (2, h // 2, h // 2),
-            (3, 0, w),
-        )
+        ) + tuple((2, t * (h // 4), h // 4) for t in range(4))
         self.scatters = (
             (3, 0, w),
             (2, 0, h),
@@ -118,7 +116,7 @@
     lengths,
     x_ref,
     cot_any,
-    vec_ref,
+    vec_refs,
     wq_any,
     wo_any,
     wu_any,
@@ -149,6 +147,7 @@
     gmid,
     gone,
     vecs,
+    vec_ref,
     vgot,
     vsum,
     vstage,
@@ -211,6 +210,11 @@
         )
     pl.semaphore_wait(barrier, dp + seq - 2)
 
+    vec_ref[...] = jnp.zeros_like(vec_ref)
+    for k, ref in enumerate(vec_refs):
+        lanes = ref.shape[1]
+        for row in range(ref.shape[0]):
+            vec_ref[k : k + 1, row * lanes : (row + 1) * lanes] = ref[row : row + 1, :].astype(f32)
     vec_sends = []
     for step in range(1, dp):
         vec_sends.append(
@@ -227,30 +231,18 @@
 
     sources = (wq_any, wo_any, wu_any, wd_any)
     weights = (wq, wo, wu, wd)
-    parity = lax.rem(z, 2)
     nk = len(peers)
 
     class Gather:
         def __init__(self, item):
             index, first, columns = s.gathers[item]
             self.buffer, self.source = weights[index], sources[index]
-            self.half, self.quarter = columns // 2, columns // 4
-            self.mine = first + parity * self.half
-            self.other = first + (1 - parity) * self.half
+            self.columns = pl.ds(first, columns)
             self.send, self.recv, self.local = g_send.at[item], g_recv.at[item], g_local.at[item]
 
-        def columns(self, first, size):
-            return pl.ds(pl.multiple_of(first, LANES), size)
-
-        def part(self, owner, first, size):
-            return self.buffer.at[owner // 2, lax.rem(owner, 2), :, self.columns(first, size)]
-
-        def both(self, first, size, which):
-            return self.buffer.at[:, which, :, self.columns(first, size)]
-
         def start(self):
-            src = self.source.at[:, self.columns(self.mine, self.half)]
-            dst = self.part(me, self.mine, self.half)
+            src = self.source.at[:, self.columns]
+            dst = self.buffer.at[chip, core, :, self.columns]
             self.own = pltpu.make_async_copy(src, dst, self.local)
             self.own.start()
             self.plane = [
@@ -260,54 +252,20 @@
             for copy in self.plane:
                 copy.start()
 
-        def middle(self):
+        def hand_on(self):
             self.own.wait()
             for copy in self.plane:
                 copy.wait_recv()
-            mine, size = self.mine, self.quarter
-            self.along = [
-                remote(
-                    self.both(mine + k * size, size, core),
-                    self.both(mine + k * size, size, core),
-                    self.send.at[nk + k],
-                    self.recv.at[nk + k],
-                    (me, (z_up, z_down)[k]),
-                )
-                for k in range(2)
-            ]
-            for copy in self.along:
-                copy.start()
-            self.across = [
-                remote(
-                    self.both(mine, self.half, core),
-                    self.both(mine, self.half, core),
-                    self.send.at[nk + 2],
-                    self.recv.at[nk + 2],
-                    sibling,
-                )
-            ]
-            self.across[0].start()
-
-        def late(self):
-            size = self.quarter
-            for k in range(2):
-                there = self.both(self.other + k * size, size, core)
-                remote(there, there, self.send.at[nk + k], self.recv.at[nk + k], sibling).wait_recv()
-                copy = remote(there, there, self.send.at[nk + 3 + k], self.recv.at[nk + 3 + k], sibling)
-                copy.start()
-                self.across.append(copy)
+            mine = self.buffer.at[:, core, :, self.columns]
+            self.across = remote(mine, mine, self.send.at[nk], self.recv.at[nk], sibling)
+            self.across.start()
 
         def finish(self):
-            there = self.both(self.mine, self.half, 1 - core)
-            remote(there, there, self.send.at[nk + 2], self.recv.at[nk + 2], sibling).wait_recv()
-            for k in range(2):
-                there = self.both(self.other + k * self.quarter, self.quarter, 1 - core)
-                remote(
-                    there, there, self.send.at[nk + 3 + k], self.recv.at[nk + 3 + k], sibling
-                ).wait_recv()
+            theirs = self.buffer.at[:, 1 - core, :, self.columns]
+            remote(theirs, theirs, self.send.at[nk], self.recv.at[nk], sibling).wait_recv()
 
         def drain(self):
-            for copy in self.plane + self.along + self.across:
+            for copy in self.plane + [self.across]:
                 copy.wait_send()
 
     gathers = [Gather(item) for item in range(len(s.gathers))]
@@ -404,13 +362,16 @@
 
     lax.fori_loop(0, s.chunks, norm_body, 0)
 
+    get_q, get_k, get_v, get_down, get_out = gathers[:5]
+    get_up = gathers[5:]
+    get_q.hand_on()
+    get_down.start()
+    get_k.hand_on()
+    get_out.start()
     for item in range(3):
-        gathers[item].middle()
-    for item in range(3, len(gathers)):
-        gathers[item].start()
-    for item in range(3):
-        gathers[item].late()
-    for item in range(3):
+        if item == 1:
+            get_v.hand_on()
+            get_up[0].start()
         gathers[item].finish()
         weight = wq[:, :, :, item * width : (item + 1) * width].reshape(width, width)
         if item < 2:
@@ -434,6 +395,10 @@
     for p in range(s.pairs):
         state[p] = jnp.zeros((LANES, 2 * LANES), f32)
 
+    def state_at(c, p):
+        first = pl.multiple_of(c * (s.pairs // 2 * LANES), LANES) + p // 2 * LANES
+        return pl.ds(first, LANES), slice(p % 2 * 2 * LANES, (p % 2 + 1) * 2 * LANES)
+
     def state_body(c, carry):
         here = span(c, CHUNK)
         keep = same(ending(c), before(c))
@@ -441,7 +406,7 @@
         for p in range(s.pairs):
             wide = jnp.concatenate([cut(here, 2, p) * chosen, chosen], axis=1)
             now = state[p]
-            state_in[c, p] = now
+            state_in[state_at(c, p)] = now
             state[p] = keep * now + tn(cut(here, 1, p), wide) * block_diag
         return carry
 
@@ -519,7 +484,6 @@
                 message(slot, step, forward).wait_send()
 
     send_states(0, True)
-    gathers[3].middle()
 
     def inside_body(c, carry):
         here = span(c, CHUNK)
@@ -536,9 +500,31 @@
         return carry
 
     lax.fori_loop(0, s.chunks, inside_body, 0)
-    gathers[3].late()
-    for item in range(4, len(gathers)):
-        gathers[item].middle()
+    get_down.hand_on()
+    get_up[1].start()
+    get_out.hand_on()
+    get_up[2].start()
+    get_down.finish()
+    cot_copy.wait()
+
+    tile = hidden // 4
+    tall = s.weights[0][0]
+    per = chips // 4
+    blocks = TALL // (2 * tall)
+
+    def hidden_body(c, carry):
+        here = span(c, TALL)
+        branch = cot[here, :]
+        collect(7, 0, branch.astype(f32))
+        for t in range(4):
+            down = wd[t * per : (t + 1) * per].reshape(tile, width)
+            grad = nt(branch, down).astype(bf16).reshape(blocks, 2, tall, tile)
+            hgrad[span(c, blocks), :, :, t * tile : (t + 1) * tile] = grad
+        return carry
+
+    lax.fori_loop(0, rows // TALL, hidden_body, 0)
+    get_up[0].hand_on()
+    get_up[3].start()
     take_states(0, True)
 
     def join_body(c, carry):
@@ -546,7 +532,7 @@
         live = in_segment(c, before(c))
         carried = same(before(c), prior)
         for p in range(s.pairs):
-            whole = state_in[c, p] + carried * state[p]
+            whole = state_in[state_at(c, p)] + carried * state[p]
             upper = whole.astype(bf16)
             lower = (whole - upper.astype(f32)).astype(bf16)
             state_b[c, p, :LANES] = upper
@@ -564,60 +550,69 @@
         return carry
 
     lax.fori_loop(0, s.chunks, join_body, 0)
-    gathers[3].finish()
-    for item in range(4, len(gathers)):
-        gathers[item].late()
-    for item in range(4, len(gathers)):
-        gathers[item].finish()
-    cot_copy.wait()
+    get_out.finish()
+    get_up[1].hand_on()
 
     bias_out, gain_two, shift_two = (vecs[k : k + 1, :width] for k in (3, 4, 5))
     bias_down = vecs[7:8, :width]
-    tile = 512
-    tall = s.weights[0][0]
-
-    def forward_body(c, carry):
+    total = state_in
+
+    def middle_of(here):
+        projected = nn(heard[here, :], wo[...].reshape(width, width))
+        return x_ref[here, :].astype(f32) + projected + bias_out
+
+    def middle_body(c, carry):
         here = span(c, TALL)
-        middle = (
-            x_ref[here, :].astype(f32)
-            + nn(heard[here, :], wo[...].reshape(width, width))
-            + bias_out
-        )
-        hat, scale = normalised(middle)
-        normed = (hat * gain_two + shift_two).astype(bf16)
-        n2t[:, here] = normed.T
-        branch = cot[here, :]
-        collect(7, 0, branch.astype(f32))
-        total = middle + bias_down
-        back = jnp.zeros((TALL, width), f32)
-        for t in range(hidden // tile):
-            cols = slice(t * tile, (t + 1) * tile)
+        middle = middle_of(here)
+        hat, _ = normalised(middle)
+        n2t[:, here] = (hat * gain_two + shift_two).astype(bf16).T
+        total[here, :] = middle + bias_down
+        return carry
+
+    lax.fori_loop(0, rows // TALL, middle_body, 0)
+
+    for t in range(4):
+        if t == 1:
+            get_up[2].hand_on()
+        if t == 2:
+            get_up[3].hand_on()
+        get_up[t].finish()
+        cols = slice(t * tile, (t + 1) * tile)
+
+        def hidden_pass(c, carry):
+            here = span(c, TALL)
             up = wu[:, :, :, cols].reshape(width, tile)
-            per = chips * tile // hidden
             down = wd[t * per : (t + 1) * per].reshape(tile, width)
-            active, slope = gelu_pair(nn(normed, up) + vecs[6:7, cols])
+            active, slope = gelu_pair(tn(n2t[:, here], up) + vecs[6:7, cols])
             active = active.astype(bf16)
             act[here, cols] = active
-            grad = (slope * nt(branch, down)).astype(bf16)
-            hgrad[span(c, TALL // (2 * tall)), :, :, cols] = grad.reshape(TALL // (2 * tall), 2, tall, tile)
+            there = (span(c, blocks), slice(None), slice(None), cols)
+            grad = (slope * hgrad[there].reshape(TALL, tile).astype(f32)).astype(bf16)
+            hgrad[there] = grad.reshape(blocks, 2, tall, tile)
             collect(6, t * tile, grad.astype(f32))
-            total = total + nn(active, down)
-            back = back + nt(grad, up)
-        out_any_rows = total.astype(bf16)
-        gone[here, :] = out_any_rows
-        copy = pltpu.make_async_copy(gone.at[here, :], out_any.at[here, :], io_sem.at[1])
-        copy.start()
+            total[here, :] += nn(active, down)
+            back = nt(grad, up)
+            gmid[here, :] = back if t == 0 else gmid[here, :] + back
+            return carry
+
+        lax.fori_loop(0, rows // TALL, hidden_pass, 0)
+
+    def output_copy(c):
+        here = span(c, TALL)
+        return pltpu.make_async_copy(gone.at[here, :], out_any.at[here, :], io_sem.at[1 + c])
+
+    def second_body(c, carry):
+        here = span(c, TALL)
+        gone[here, :] = total[here, :].astype(bf16)
+        output_copy(c).start()
+        hat, scale = normalised(middle_of(here))
+        back = gmid[here, :]
         collect(4, 0, back * hat)
         collect(5, 0, back)
-        grad_middle = branch.astype(f32) + norm_back(back, gain_two, hat, scale)
-        gmid[here, :] = grad_middle
-        copy.wait()
-        low = grad_middle.astype(bf16)
-        gone[here, :] = low
-        collect(3, 0, low.astype(f32))
-        return carry
-
-    lax.fori_loop(0, rows // TALL, forward_body, 0)
+        gmid[here, :] = cot[here, :].astype(f32) + norm_back(back, gain_two, hat, scale)
+        return carry
+
+    lax.fori_loop(0, rows // TALL, second_body, 0)
     for gather in gathers:
         gather.drain()
 
@@ -632,11 +627,12 @@
             self.cols = pl.ds(first, columns)
             shared = item - len(s.scatters) + 3
             if shared >= 0:
-                here = pl.ds(shared * self.height, self.height)
-                self.rb0, self.rb1 = rb0[0].at[:, here], rb1[0].at[:, here]
+                self.rb0 = rb0[0].at[:, pl.ds(shared * self.height, self.height)]
             else:
-                self.rb0, self.rb1 = rb0[item], rb1[item]
+                self.rb0 = rb0[item]
+            self.rb1 = rb1[item]
             self.zsrc, self.zr1, self.zr2 = zsrc[item], zr1[item], zr2[item]
+            self.part = columns // seq
             self.send, self.recv = r_send.at[item], r_recv.at[item]
 
         def start(self):
@@ -673,23 +669,6 @@
             for copy in self.sends:
                 copy.start()
 
-        def exchange(self, source, target, base, swap):
-            half = self.count // 2
-            partners = (z + 1 - 2 * parity, seq - 1 - z)
-            copies = [
-                remote(
-                    source.at[:, k * half : (k + 1) * half],
-                    target.at[:, k * half : (k + 1) * half],
-                    self.send.at[base + k],
-                    self.recv.at[base + k],
-                    (me, partners[1 - k if swap else k]),
-                )
-                for k in range(2)
-            ]
-            for copy in copies:
-                copy.start()
-            return copies
-
         def along(self):
             for copy in self.sends:
                 copy.wait_recv()
@@ -697,24 +676,54 @@
             for k in range(nk):
                 total = total + self.rb1[k].astype(f32)
             self.zsrc[...] = total.astype(bf16)
-            self.first_pair = self.exchange(self.zsrc, self.zr1, nk + 1, False)
+            self.first = []
+            for step in range(1, seq):
+                target = lax.rem(z + step, seq)
+                copy = remote(
+                    self.zsrc.at[:, span(target, self.part)],
+                    self.zr1.at[step - 1],
+                    self.send.at[nk + step],
+                    self.recv.at[nk + step],
+                    (me, target),
+                )
+                copy.start()
+                self.first.append(copy)
 
         def along_again(self):
-            for copy in self.first_pair:
-                copy.wait()
-            self.zsrc[...] = (self.zsrc[...].astype(f32) + self.zr1[...].astype(f32)).astype(bf16)
-            self.second_pair = self.exchange(self.zsrc, self.zr2, nk + 3, True)
+            for copy in self.first:
+                copy.wait_recv()
+            mine = span(z, self.part)
+            total = self.zsrc[:, mine].astype(f32)
+            for step in range(seq - 1):
+                total = total + self.zr1[step].astype(f32)
+            self.zr2[:, mine] = total.astype(bf16)
+            self.second = []
+            for step in range(1, seq):
+                copy = remote(
+                    self.zr2.at[:, mine],
+                    self.zr2.at[:, mine],
+                    self.send.at[nk + seq - 1 + step],
+                    self.recv.at[nk + seq - 1 + step],
+                    (me, lax.rem(z + step, seq)),
+                )
+                copy.start()
+                self.second.append(copy)
 
         def finish(self):
-            for copy in self.second_pair:
-                copy.wait_recv()
-            self.result[:, self.cols] = (
-                self.zsrc[...].astype(f32) + self.zr2[...].astype(f32)
-            ).astype(bf16)
+            for step in range(1, seq):
+                theirs = self.zr2.at[:, span(lax.rem(z - step + seq, seq), self.part)]
+                remote(
+                    theirs,
+                    theirs,
+                    self.send.at[nk + seq - 1 + step],
+                    self.recv.at[nk + seq - 1 + step],
+                    sibling,
+                ).wait_recv()
+            self.result[:, self.cols] = self.zr2[...]
 
         def drain(self):
             self.across.wait_send()
-            for copy in self.sends + self.second_pair:
+            for copy in self.sends + self.first + self.second:
                 copy.wait_send()
 
     scatters = [Scatter(item) for item in range(len(s.scatters))]
@@ -722,7 +731,6 @@
     qkv_items = scatters[3:]
 
     def down_body(c, carry):
-        per = chips * tile // hidden
         grad = tn(act[:, span(c, tile)], cot[...]).astype(bf16)
         wd[pl.ds(c * per, per)] = grad.reshape(per, 2, hidden // dp, width)
         return carry
@@ -736,7 +744,10 @@
 
     def heads_body(c, carry):
         here = span(c, CHUNK)
-        back = nt(gone[here, :], wo[...].reshape(width, width)).astype(bf16).astype(f32)
+        low = gmid[here, :].astype(bf16)
+        gone[here, :] = low
+        collect(3, 0, low.astype(f32))
+        back = nt(low, wo[...].reshape(width, width)).astype(bf16).astype(f32)
         for p in range(s.pairs):
             first = 2 * p * LANES
             result = acc[here, first : first + LANES]
@@ -755,6 +766,8 @@
             ).astype(bf16)
         return carry
 
+    for c in range(rows // TALL):
+        output_copy(c).wait()
     lax.fori_loop(0, s.chunks, heads_body, 0)
 
     def grads_of(here, p):
@@ -771,7 +784,7 @@
         live = in_segment(c, before(c)).astype(bf16)
         for p in range(s.pairs):
             now = state[p]
-            state_in[c, p] = now
+            state_in[state_at(c, p)] = now
             wide = jnp.concatenate(grads_of(here, p), axis=1)
             state[p] = keep * now + tn(cut(here, 0, p) * live, wide) * block_diag
         return carry
@@ -812,7 +825,7 @@
             v_high = jnp.concatenate([v * ones_high, ones_high], axis=1)
             q_low, q_high = q * ones_low, q * ones_high
             dn_low, dn_high = dn * ones_low, dn * ones_high
-            ahead = state_in[c, p] + carried * state[p]
+            ahead = state_in[state_at(c, p)] + carried * state[p]
             sums = ahead[:, LANES:]
             sums = 2.0 * spread_ends(sums + pltpu.roll(sums, 64, 1)) * block_diag[:, LANES:]
             upper = sums.astype(bf16).astype(f32)
@@ -861,8 +874,8 @@
         hat, scale = normalised(x_ref[here, :].astype(f32))
         collect(0, 0, grad * hat)
         collect(1, 0, grad)
-        gmid[here, :] = gmid[here, :] + norm_back(grad, gain_one, hat, scale)
-        pltpu.make_async_copy(gmid.at[here, :], gin_any.at[here, :], io_sem.at[2 + c]).start()
+        gone[here, :] = (gmid[here, :] + norm_back(grad, gain_one, hat, scale)).astype(bf16)
+        pltpu.make_async_copy(gone.at[here, :], gin_any.at[here, :], io_sem.at[1 + rows // TALL + c]).start()
         return carry
 
     lax.fori_loop(0, rows // TALL, input_body, 0)
@@ -925,13 +938,68 @@
 
     for c in range(rows // TALL):
         here = pl.ds(c * TALL, TALL)
-        pltpu.make_async_copy(gmid.at[here, :], gin_any.at[here, :], io_sem.at[2 + c]).wait()
+        pltpu.make_async_copy(gone.at[here, :], gin_any.at[here, :], io_sem.at[1 + rows // TALL + c]).wait()
     drain_states(0, True)
     drain_states(1, False)
     for copy in vec_sends + vec_back + vec_z:
         copy.wait_send()
     for item in scatters:
         item.drain()
+
+
+def widen_kernel(parts, *refs):
+    count = 7
+    ins, outs = refs[:count], refs[count : count + 14]
+    got, made, in_sem, out_sem = refs[count + 14 :]
+    out_in, gin_in, *grads_in, vec_in = ins
+    out_out, gin_out, *rest = outs
+    rows = out_in.shape[0] // parts
+    here = [pl.ds(k * rows, rows) for k in range(parts)]
+    loads = [
+        [pltpu.make_async_copy(source.at[at], got.at[i, at], in_sem.at[i, k]) for k, at in enumerate(here)]
+        for i, source in enumerate((gin_in, out_in))
+    ]
+    for copy in loads[0] + loads[1]:
+        copy.start()
+    stores = []
+    for k, at in enumerate(here):
+        loads[0][k].wait()
+        made[at] = got[0, at].astype(f32)
+        stores.append(pltpu.make_async_copy(made.at[at], gin_out.at[at], out_sem.at[0, k]))
+        stores[-1].start()
+    for k, at in enumerate(here):
+        loads[1][k].wait()
+        stores.append(pltpu.make_async_copy(got.at[1, at], out_out.at[at], out_sem.at[1, k]))
+        stores[-1].start()
+    for grad, result in zip(grads_in, rest[:4]):
+        result[...] = grad[...].astype(f32)
+    for k, result in enumerate(rest[4:]):
+        result[...] = vec_in[k : k + 1, : result.shape[1]]
+    for copy in stores:
+        copy.wait()
+
+
+def widen(s, vectors, results):
+    parts = 4
+    out, gin, *grads, vec = results
+    vmem = pl.BlockSpec(memory_space=pltpu.VMEM)
+    anywhere = pl.BlockSpec(memory_space=pl.ANY)
+    return pl.pallas_call(
+        functools.partial(widen_kernel, parts),
+        out_shape=[jax.ShapeDtypeStruct(out.shape, bf16)]
+        + [jax.ShapeDtypeStruct(value.shape, f32) for value in (gin, *grads)]
+        + [jax.ShapeDtypeStruct((1, v.shape[0]), f32) for v in vectors],
+        in_specs=[anywhere] * 2 + [vmem] * 5,
+        out_specs=[anywhere] * 2 + [vmem] * 12,
+        scratch_shapes=[
+            pltpu.VMEM((2,) + out.shape, bf16),
+            pltpu.VMEM(out.shape, f32),
+            pltpu.SemaphoreType.DMA((2, parts)),
+            pltpu.SemaphoreType.DMA((2, parts)),
+        ],
+        compiler_params=pltpu.CompilerParams(vmem_limit_bytes=63 << 20),
+        name="widen",
+    )(out, gin, *grads, vec)
 
 
 def solution(mesh):
@@ -943,9 +1011,6 @@
         dp, seq, chips, pairs = s.dp, s.seq, s.chips, s.pairs
         nk = chips - 1
         vectors = (gain_one, shift_one, b_qk, b_out, gain_two, shift_two, b_up, b_down)
-        vec = jnp.stack(
-            [jnp.pad(v.astype(f32), (0, s.vec_lanes - v.shape[0])) for v in vectors]
-        )
         vmem = pl.BlockSpec(memory_space=pltpu.VMEM)
         anywhere = pl.BlockSpec(memory_space=pl.ANY)
         grids = [(chips, 2) + shape for shape in s.weights]
@@ -961,7 +1026,7 @@
                 pltpu.VMEM((rows, 3 * width), bf16),
                 pltpu.VMEM((rows, 2 * width), f32),
                 pltpu.VMEM((s.chunks, CHUNK, CHUNK), bf16),
-                pltpu.VMEM((s.chunks, pairs, LANES, 2 * LANES), f32),
+                pltpu.VMEM((rows, width), f32),
                 pltpu.VMEM((pairs, LANES, 2 * LANES), f32),
                 pltpu.VMEM((s.chunks, pairs, 2 * LANES, 2 * LANES), bf16),
                 pltpu.VMEM((width, rows), bf16),
@@ -970,6 +1035,7 @@
                 pltpu.VMEM((rows, width), f32),
                 pltpu.VMEM((rows, width), bf16),
                 pltpu.VMEM((8, hidden), f32),
+                pltpu.VMEM((8, s.vec_lanes), f32),
                 pltpu.VMEM((dp, 8, s.vec_lanes), f32),
                 pltpu.VMEM((8, sum(s.sizes)), f32),
                 pltpu.VMEM((dp, 8, s.vec_lanes), f32),
@@ -979,31 +1045,31 @@
                 pltpu.VMEM((2, pairs // 2 + 1, LANES, LANES), bf16),
                 pltpu.VMEM((2, seq - 1, pairs // 2 + 1, LANES, LANES), bf16),
                 [pltpu.VMEM((chips,) + shape, bf16) for shape in shapes[:3]],
-                [pltpu.VMEM((nk,) + shape, bf16) for shape in shapes[:3]],
+                [pltpu.VMEM((nk,) + shape, bf16) for shape in shapes],
                 [pltpu.VMEM(shape, bf16) for shape in shapes],
-                [pltpu.VMEM(shape, bf16) for shape in shapes],
+                [pltpu.VMEM((seq - 1, tall_, n // seq), bf16) for tall_, n in shapes],
                 [pltpu.VMEM(shape, bf16) for shape in shapes],
                 dma((len(s.gathers),)),
-                dma((len(s.gathers), nk + 5)),
-                dma((len(s.gathers), nk + 5)),
+                dma((len(s.gathers), nk + 1)),
+                dma((len(s.gathers), nk + 1)),
                 dma((2 * dp - 2 + seq - 1,)),
                 dma((2 * dp - 2 + seq - 1,)),
                 dma((2, seq - 1)),
                 dma((2, seq - 1)),
-                dma((len(s.scatters), nk + 5)),
-                dma((len(s.scatters), nk + 5)),
-                dma((2 + rows // TALL,)),
+                dma((len(s.scatters), nk + 2 * seq - 1)),
+                dma((len(s.scatters), nk + 2 * seq - 1)),
+                dma((1 + 2 * (rows // TALL),)),
             ]
         )
         outs = pl.pallas_call(
             functools.partial(kernel, s),
             out_shape=(
                 jax.ShapeDtypeStruct((rows, width), bf16),
-                jax.ShapeDtypeStruct((rows, width), f32),
+                jax.ShapeDtypeStruct((rows, width), bf16),
             )
             + tuple(jax.ShapeDtypeStruct(shape, bf16) for shape in s.weights)
             + (jax.ShapeDtypeStruct((8, s.vec_lanes), f32),),
-            in_specs=[pl.BlockSpec(memory_space=pltpu.SMEM), vmem, anywhere, vmem]
+            in_specs=[pl.BlockSpec(memory_space=pltpu.SMEM), vmem, anywhere, [vmem] * 8]
             + [anywhere] * 4,
             out_specs=(anywhere, anywhere) + (vmem,) * 5,
             scratch_shapes=scratch,
@@ -1015,28 +1081,29 @@
             lengths.reshape(3),
             inputs.reshape(rows, width),
             cotangent.reshape(rows, width),
-            vec,
+            [v.reshape(-1, min(v.shape[0], LANES)) for v in vectors],
             w_qkv,
             w_out,
             w_up,
             w_down,
         )
-        out, gin, g_qkv, g_out, g_up, g_down, g_vec = outs
-        pieces = [g_vec[k, : v.shape[0]] for k, v in enumerate(vectors)]
+        out, gin, *grads = widen(s, vectors, outs)
+        g_qkv, g_out, g_up, g_down, *pieces = grads
+        pieces = [piece.reshape(piece.shape[1]) for piece in pieces]
         return (
             out.reshape(inputs.shape),
             gin.reshape(inputs.shape),
             pieces[0],
             pieces[1],
-            g_qkv.astype(f32),
+            g_qkv,
             pieces[2],
-            g_out.astype(f32),
+            g_out,
             pieces[3],
             pieces[4],
             pieces[5],
-            g_up.astype(f32),
+            g_up,
             pieces[6],
-            g_down.astype(f32),
+            g_down,
             pieces[7],
         )
 

time: 185 us -> 146 us (0.79)
  Pallas kernels: 166 us -> 145 us
  local copies, waits for them, and re-layouts: 12.9 us -> 0 us
  other arithmetic: 5.62 us -> 0 us
    pallas_call x1, Pallas kernels: 166 us -> 140 us  [body(): pl.pallas_call(functools.partial(kernel, s), out_shape=(jax.ShapeDtypeStr...]
    pallas_call x0 -> x1, Pallas kernels: none -> 5.41 us  [widen(): pl.pallas_call(functools.partial(widen_kernel, parts), out_shape=[jax.Sha...]
    convert_element_type x4 -> x0, other arithmetic: 5.02 us -> none  [the longest x1 1.8 us: body(): g_down.astype(f32)]
    pad x7 -> x0, local copies, waits for them, and re-layouts: 4.62 us -> none  [body(): jnp.pad(v.astype(f32), (0, s.vec_lanes - v.shape[0]))]
    unnamed x10 -> x0, local copies, waits for them, and re-layouts: 3.72 us -> none
    squeeze x2 -> x0, local copies, waits for them, and re-layouts: 2.61 us -> none  [body(): pieces = [g_vec[k, :v.shape[0]] for k, v in enumerate(vectors)]]
where the time goes in v2:
time: 146 us
  Pallas kernels  145 us (99%)
    pallas_call x1, Pallas kernels, body(): pl.pallas_call(functools.partial(kernel, s), out_shape=(jax.ShapeDtypeStr...  140 us
    pallas_call x1, Pallas kernels, widen(): pl.pallas_call(functools.partial(widen_kernel, parts), out_shape=[jax.Sha...  5.41 us

profile of v2, /device:TPU:0, one launch (start us, length us, event | category | flops | bytes accessed | tf_op | source)
XLA Modules:
  0.0 145.9 jit_solution(1478659226269563847)
XLA Ops:
  0.7 139.6 %layer.1 = (bf16[1280,512]{1,0:T(8,128)(2,1)}, bf16[1280,512]{1,0:T(8,128)(2,1)}, bf16[64,1536]{1,0:T(8,128)(2,1)}, bf16[64,512]{1,0:T(8,128)(2,1)}, bf16[64,204...) custom-call(s32[3]{0:T(128)} %bitcast.23, bf16[1280,512]{1,0:T(8,128)(2,1)} %bitcast.21, ...), custom_call_target="tpu_custom_call" | custom-call | tf_op jit(solution)/shard_map/layer/pallas_call | solution.py:1064
  140.3 5.4 %widen.1 = (bf16[1280,512]{1,0:T(8,128)(2,1)}, f32[1280,512]{1,0:T(8,128)}, f32[64,1536]{1,0:T(8,128)}, f32[64,512]{1,0:T(8,128)}, f32[64,2048]{1,0:T(8,128)}, /...) custom-call(bf16[1280,512]{1,0:T(8,128)(2,1)} %get-tuple-element.35., ...), custom_call_target="tpu_custom_call" | custom-call | tf_op jit(solution)/shard_map/widen/pallas_call | solution.py:987

commit v3 on v2

--- a/solution.py
+++ b/solution.py
@@ -69,16 +69,8 @@
 
 
 def gelu_pair(x):
-    e = jnp.exp(x * x * -0.5)
-    z = jnp.abs(x) * 0.7071067811865476
-    t = 1.0 / (1.0 + 0.3275911 * z)
-    poly = t * (
-        0.254829592
-        + t * (-0.284496736 + t * (1.421413741 + t * (-1.453152027 + t * 1.061405429)))
-    )
-    tail = 0.5 * poly * e
-    cdf = jnp.where(x >= 0.0, 1.0 - tail, tail)
-    return x * cdf, cdf + x * (0.3989422804014327 * e)
+    cdf = 0.5 + 0.5 * lax.erf(x * 0.7071067811865476)
+    return x * cdf, cdf + x * (0.3989422804014327 * jnp.exp2(x * x * -0.7213475204444817))
 
 
 class Shape:
@@ -95,9 +87,9 @@
         w, h, d = width, hidden, self.dp
         self.weights = ((w // d, 3 * w), (w // d, w), (w // d, h), (h // d, w))
         self.gathers = (
-            (0, 0, w),
             (0, w, w),
             (0, 2 * w, w),
+            (0, 0, w),
             (3, 0, w),
             (1, 0, w),
         ) + tuple((2, t * (h // 4), h // 4) for t in range(4))
@@ -305,6 +297,7 @@
         (lanes_of((LANES, 2 * LANES)) // 64) % 2 == rows_of((LANES, 2 * LANES)) // 64
     ).astype(f32)
     low_pair = lanes_of(pair) < 64
+    diagonal = lanes_of(pair) == rows_of(pair)
     low_half = (lanes_of(pair) & 63) < 32
     ones_low = lane_low.astype(bf16)
     ones_high = 1.0 - ones_low
@@ -362,31 +355,31 @@
 
     lax.fori_loop(0, s.chunks, norm_body, 0)
 
-    get_q, get_k, get_v, get_down, get_out = gathers[:5]
+    get_down, get_out = gathers[3:5]
     get_up = gathers[5:]
-    get_q.hand_on()
-    get_down.start()
-    get_k.hand_on()
-    get_out.start()
-    for item in range(3):
-        if item == 1:
-            get_v.hand_on()
-            get_up[0].start()
-        gathers[item].finish()
-        weight = wq[:, :, :, item * width : (item + 1) * width].reshape(width, width)
-        if item < 2:
-            bias = vecs[2:3, item * width : (item + 1) * width]
+
+    def project(get, part):
+        get.finish()
+        cols = slice(part * width, (part + 1) * width)
+        weight = wq[:, :, :, cols].reshape(width, width)
 
         def project_body(c, carry):
             here = span(c, TALL)
             mixed = nn(n1[here, :], weight)
-            if item < 2:
-                mixed = mixed + bias
+            if part < 2:
+                mixed = mixed + vecs[2:3, cols]
                 mixed = jnp.where(mixed > 0.0, mixed + 1.0, jnp.exp(jnp.minimum(mixed, 0.0)))
-            feat[here, item * width : (item + 1) * width] = mixed.astype(bf16)
+            feat[here, cols] = mixed.astype(bf16)
             return carry
 
         lax.fori_loop(0, rows // TALL, project_body, 0)
+
+    gathers[0].hand_on()
+    get_down.start()
+    gathers[1].hand_on()
+    get_out.start()
+    project(gathers[0], 1)
+    project(gathers[1], 2)
 
     def cut(here, part, p):
         first = part * width + p * LANES
@@ -424,23 +417,20 @@
             halves.append(left + pltpu.roll(left, 64, 1))
             ends.append(spread_ends(right + pltpu.roll(right, 64, 1)))
         for q in range(s.pairs // 2):
-            msg[slot, q] = jnp.where(low_pair, halves[2 * q], halves[2 * q + 1]).astype(bf16)
-        total = ends[0]
-        lanes = LANES // s.pairs
-        for p in range(1, s.pairs):
-            total = jnp.where(lanes_of(pair) // lanes == p, ends[p], total)
-        upper = total.astype(bf16).astype(f32)
-        total = jnp.where(lanes_of(pair) % lanes < lanes // 2, upper, total - upper)
-        msg[slot, s.pairs // 2] = total.astype(bf16)
+            msg[slot, q * LANES : (q + 1) * LANES] = jnp.where(
+                low_pair, halves[2 * q], halves[2 * q + 1]
+            )
+        ends = [jnp.sum(jnp.where(diagonal, end, 0.0), axis=0, keepdims=True) for end in ends]
+        ends.append(jnp.zeros((msg.shape[1] - s.pairs // 2 * LANES - s.pairs, LANES), f32))
+        msg[slot, s.pairs // 2 * LANES :] = jnp.concatenate(ends, axis=0)
 
     def unpacked(slot, step, p):
-        sums = msg_in[slot, step, p // 2].astype(f32)
+        sums = msg_in[slot, step, p // 2 * LANES : (p // 2 + 1) * LANES]
         turned = pltpu.roll(sums, 64, 1)
         left = jnp.where(low_pair, sums, turned) if p % 2 == 0 else jnp.where(low_pair, turned, sums)
-        first = p * (LANES // s.pairs)
-        middle = first + LANES // s.pairs // 2
-        ends = msg_in[slot, step, s.pairs // 2].astype(f32)
-        right = ends[:, first : first + 1] + ends[:, middle : middle + 1]
+        first = s.pairs // 2 * LANES + p
+        ends = jnp.where(diagonal, msg_in[slot, step, first : first + 1], 0.0)
+        right = jnp.sum(ends, axis=1, keepdims=True)
         return jnp.concatenate([left, jnp.broadcast_to(right, pair)], axis=1) * block_diag
 
     def message(slot, step, forward):
@@ -484,19 +474,25 @@
                 message(slot, step, forward).wait_send()
 
     send_states(0, True)
+    gathers[2].hand_on()
+    get_up[0].start()
+    project(gathers[2], 0)
 
     def inside_body(c, carry):
         here = span(c, CHUNK)
         seen = mask[c]
-        for p in range(s.pairs):
-            q, k, v = cut(here, 0, p), cut(here, 1, p), cut(here, 2, p)
-            k_low, v_low = k * ones_low, v * ones_low
-            k_high, v_high = k * ones_high, v * ones_high
-            s_low = nt(q, k_low).astype(bf16) * seen
-            s_high = nt(q, k_high).astype(bf16) * seen
+        raw = []
+        for p in range(s.pairs):
+            q, k = cut(here, 0, p), cut(here, 1, p)
+            raw.append((nt(q, k * ones_low), nt(q, k * ones_high)))
+        for p in range(s.pairs):
+            v = cut(here, 2, p)
+            scores = jnp.concatenate([part.astype(bf16) * seen for part in raw[p]], axis=1)
+            low = jnp.concatenate([v * ones_low, ones_low], axis=1)
+            high = jnp.concatenate([v * ones_high, ones_high], axis=1)
             acc[here, 2 * p * LANES : (2 * p + 2) * LANES] = nn(
-                s_low, jnp.concatenate([v_low, ones_low], axis=1)
-            ) + nn(s_high, jnp.concatenate([v_high, ones_high], axis=1))
+                scores, jnp.concatenate([low, high], axis=0)
+            )
         return carry
 
     lax.fori_loop(0, s.chunks, inside_body, 0)
@@ -579,23 +575,18 @@
         get_up[t].finish()
         cols = slice(t * tile, (t + 1) * tile)
 
-        def hidden_pass(c, carry):
-            here = span(c, TALL)
-            up = wu[:, :, :, cols].reshape(width, tile)
-            down = wd[t * per : (t + 1) * per].reshape(tile, width)
-            active, slope = gelu_pair(tn(n2t[:, here], up) + vecs[6:7, cols])
-            active = active.astype(bf16)
-            act[here, cols] = active
-            there = (span(c, blocks), slice(None), slice(None), cols)
-            grad = (slope * hgrad[there].reshape(TALL, tile).astype(f32)).astype(bf16)
-            hgrad[there] = grad.reshape(blocks, 2, tall, tile)
-            collect(6, t * tile, grad.astype(f32))
-            total[here, :] += nn(active, down)
-            back = nt(grad, up)
-            gmid[here, :] = back if t == 0 else gmid[here, :] + back
-            return carry
-
-        lax.fori_loop(0, rows // TALL, hidden_pass, 0)
+        up = wu[:, :, :, cols].reshape(width, tile)
+        down = wd[t * per : (t + 1) * per].reshape(tile, width)
+        active, slope = gelu_pair(tn(n2t[...], up) + vecs[6:7, cols])
+        active = active.astype(bf16)
+        act[:, cols] = active
+        grad = slope * hgrad[:, :, :, cols].reshape(rows, tile).astype(f32)
+        grad = grad.astype(bf16)
+        hgrad[:, :, :, cols] = grad.reshape(rows // (2 * tall), 2, tall, tile)
+        collect(6, t * tile, grad.astype(f32))
+        total[...] += nn(active, down)
+        back = nt(grad, up)
+        gmid[...] = back if t == 0 else gmid[...] + back
 
     def output_copy(c):
         here = span(c, TALL)
@@ -635,28 +626,17 @@
             self.part = columns // seq
             self.send, self.recv = r_send.at[item], r_recv.at[item]
 
-        def start(self):
-            self.across = remote(
+        def across(self):
+            return remote(
                 self.stage.at[pl.ds(0, chips), 1 - core, :, self.cols],
                 self.rb0,
                 self.send.at[0],
                 self.recv.at[0],
                 sibling,
             )
-            self.across.start()
-
-        def plane(self):
-            self.across.wait_recv()
-
-            def add(k, carry):
-                here = (k, core, slice(None), self.cols)
-                self.stage[here] = (
-                    self.stage[here].astype(f32) + self.rb0[k].astype(f32)
-                ).astype(bf16)
-                return carry
-
-            lax.fori_loop(0, chips, add, 0)
-            self.sends = [
+
+        def sends(self):
+            return [
                 remote(
                     self.stage.at[peer[0] // 2, core, :, self.cols],
                     self.rb1.at[k],
@@ -666,69 +646,78 @@
                 )
                 for k, peer in enumerate(peers)
             ]
-            for copy in self.sends:
+
+        def quarters(self):
+            return [
+                remote(
+                    self.zsrc.at[:, span(lax.rem(z + step, seq), self.part)],
+                    self.zr1.at[step - 1],
+                    self.send.at[nk + step],
+                    self.recv.at[nk + step],
+                    (me, lax.rem(z + step, seq)),
+                )
+                for step in range(1, seq)
+            ]
+
+        def totals(self, arriving=False):
+            copies = []
+            for step in range(1, seq):
+                owner = lax.rem(z - step + seq, seq) if arriving else z
+                piece = self.zr2.at[:, span(owner, self.part)]
+                k = nk + seq - 1 + step
+                target = (me, lax.rem(z + step, seq))
+                copies.append(remote(piece, piece, self.send.at[k], self.recv.at[k], target))
+            return copies
+
+        def start(self):
+            self.across().start()
+
+        def plane(self):
+            self.across().wait_recv()
+
+            def add(k, carry):
+                here = (k, core, slice(None), self.cols)
+                self.stage[here] = (
+                    self.stage[here].astype(f32) + self.rb0[k].astype(f32)
+                ).astype(bf16)
+                return carry
+
+            lax.fori_loop(0, chips, add, 0)
+            for copy in self.sends():
                 copy.start()
 
         def along(self):
-            for copy in self.sends:
+            for copy in self.sends():
                 copy.wait_recv()
             total = self.stage[chip, core, :, self.cols].astype(f32)
             for k in range(nk):
                 total = total + self.rb1[k].astype(f32)
             self.zsrc[...] = total.astype(bf16)
-            self.first = []
-            for step in range(1, seq):
-                target = lax.rem(z + step, seq)
-                copy = remote(
-                    self.zsrc.at[:, span(target, self.part)],
-                    self.zr1.at[step - 1],
-                    self.send.at[nk + step],
-                    self.recv.at[nk + step],
-                    (me, target),
-                )
+            for copy in self.quarters():
                 copy.start()
-                self.first.append(copy)
 
         def along_again(self):
-            for copy in self.first:
+            for copy in self.quarters():
                 copy.wait_recv()
             mine = span(z, self.part)
             total = self.zsrc[:, mine].astype(f32)
             for step in range(seq - 1):
                 total = total + self.zr1[step].astype(f32)
             self.zr2[:, mine] = total.astype(bf16)
-            self.second = []
-            for step in range(1, seq):
-                copy = remote(
-                    self.zr2.at[:, mine],
-                    self.zr2.at[:, mine],
-                    self.send.at[nk + seq - 1 + step],
-                    self.recv.at[nk + seq - 1 + step],
-                    (me, lax.rem(z + step, seq)),
-                )
+            for copy in self.totals():
                 copy.start()
-                self.second.append(copy)
 
         def finish(self):
-            for step in range(1, seq):
-                theirs = self.zr2.at[:, span(lax.rem(z - step + seq, seq), self.part)]
-                remote(
-                    theirs,
-                    theirs,
-                    self.send.at[nk + seq - 1 + step],
-                    self.recv.at[nk + seq - 1 + step],
-                    sibling,
-                ).wait_recv()
+            for copy in self.totals(True):
+                copy.wait_recv()
             self.result[:, self.cols] = self.zr2[...]
 
         def drain(self):
-            self.across.wait_send()
-            for copy in self.sends + self.first + self.second:
+            for copy in [self.across()] + self.sends() + self.quarters() + self.totals():
                 copy.wait_send()
 
     scatters = [Scatter(item) for item in range(len(s.scatters))]
     down_item, up_item, out_item = scatters[:3]
-    qkv_items = scatters[3:]
 
     def down_body(c, carry):
         grad = tn(act[:, span(c, tile)], cot[...]).astype(bf16)
@@ -789,9 +778,9 @@
             state[p] = keep * now + tn(cut(here, 0, p) * live, wide) * block_diag
         return carry
 
+    down_item.plane()
     lax.fori_loop(0, s.chunks, gstate_body, 0)
     send_states(1, False)
-    down_item.plane()
 
     def up_body(c, carry):
         cols = span(c, tile)
@@ -803,70 +792,114 @@
     up_item.start()
     wo[...] = tn(heard[...], gone[...]).astype(bf16).reshape(chips, 2, width // dp, width)
     out_item.start()
-    down_item.along()
     up_item.plane()
     out_item.plane()
-    down_item.along_again()
+
+    q_item, k_item, v_item = scatters[3:]
+
+    def projection_grad(part):
+        cols = slice(part * width, (part + 1) * width)
+        grad = nn(n1t[...], act[:, cols]).astype(bf16)
+        stage_q[:chips, :, :, cols] = grad.reshape(chips, 2, width // dp, width)
+
+    def value_body(c, carry):
+        here = span(c, CHUNK)
+        seen_t = mask[c].T
+        raw = []
+        for p in range(s.pairs):
+            q, k = cut(here, 0, p), cut(here, 1, p)
+            raw.append((nt(k * ones_low, q), nt(k * ones_high, q)))
+        for p in range(s.pairs):
+            dn, _ = grads_of(here, p)
+            scores = jnp.concatenate([part.astype(bf16) * seen_t for part in raw[p]], axis=1)
+            acc[here, p * LANES : (p + 1) * LANES] = nn(
+                scores, jnp.concatenate([dn * ones_low, dn * ones_high], axis=0)
+            )
+        return carry
+
+    lax.fori_loop(0, s.chunks, value_body, 0)
     take_states(1, False)
 
-    def back_body(c, carry):
+    def ahead_body(c, carry):
         here = span(c, CHUNK)
-        seen = mask[c]
-        seen_t = seen.T
-        live = in_segment(c, before(c))
         chosen = in_segment(c, ending(c))
         carried = same(ending(c), last)
         for p in range(s.pairs):
-            q, k, v = cut(here, 0, p), cut(here, 1, p), cut(here, 2, p)
-            dn, dd = grads_of(here, p)
-            wide = jnp.concatenate([dn, dd], axis=1)
-            k_low, k_high = k * ones_low, k * ones_high
-            v_low = jnp.concatenate([v * ones_low, ones_low], axis=1)
-            v_high = jnp.concatenate([v * ones_high, ones_high], axis=1)
-            q_low, q_high = q * ones_low, q * ones_high
-            dn_low, dn_high = dn * ones_low, dn * ones_high
             ahead = state_in[state_at(c, p)] + carried * state[p]
             sums = ahead[:, LANES:]
             sums = 2.0 * spread_ends(sums + pltpu.roll(sums, 64, 1)) * block_diag[:, LANES:]
             upper = sums.astype(bf16).astype(f32)
             sums = jnp.where(low_half, upper, sums - upper)
-            ahead = jnp.concatenate([ahead[:, :LANES], sums], axis=1).astype(bf16)
-            ds_low = nt(wide, v_low).astype(bf16) * seen
-            ds_high = nt(wide, v_high).astype(bf16) * seen
-            gq = nn(ds_low, k_low) + nn(ds_high, k_high) + live * (
-                nt(wide, state_b[c, p, :LANES]) + nt(wide, state_b[c, p, LANES:])
+            state_in[state_at(c, p)] = jnp.concatenate([ahead[:, :LANES], sums], axis=1)
+            grad = acc[here, p * LANES : (p + 1) * LANES] + chosen * nn(
+                cut(here, 1, p), ahead[:, :LANES].astype(bf16)
             )
-            dst_low = nt(v_low, wide).astype(bf16) * seen_t
-            dst_high = nt(v_high, wide).astype(bf16) * seen_t
-            v_ones = jnp.concatenate([v, jnp.ones_like(v)], axis=1)
-            gk = nn(dst_low, q_low) + nn(dst_high, q_high) + chosen * nt(v_ones, ahead)
-            st_low = nt(k_low, q).astype(bf16) * seen_t
-            st_high = nt(k_high, q).astype(bf16) * seen_t
-            gv = nn(st_low, dn_low) + nn(st_high, dn_high) + chosen * nn(k, ahead[:, :LANES])
-            for part, grad in ((0, gq), (1, gk), (2, gv)):
+            first = 2 * width + p * LANES
+            act[here, first : first + LANES] = grad.astype(bf16)
+        return carry
+
+    lax.fori_loop(0, s.chunks, ahead_body, 0)
+    projection_grad(2)
+    v_item.start()
+    down_item.along()
+
+    def back_body(c, carry):
+        here = span(c, CHUNK)
+        for at, work in ((0, v_item.plane), (2, down_item.along_again), (3, up_item.along)):
+            pl.when(c == min(at, s.chunks - 1))(work)
+        seen = mask[c]
+        live = in_segment(c, before(c))
+        chosen = in_segment(c, ending(c))
+        raw = []
+        extra = []
+        for p in range(s.pairs):
+            v = cut(here, 2, p)
+            wide = jnp.concatenate(grads_of(here, p), axis=1)
+            low = jnp.concatenate([v * ones_low, ones_low], axis=1)
+            high = jnp.concatenate([v * ones_high, ones_high], axis=1)
+            raw.append((nt(wide, low), nt(wide, high)))
+            both = jnp.concatenate([v, jnp.ones_like(v)], axis=1)
+            ahead = state_in[state_at(c, p)]
+            upper = ahead.astype(bf16)
+            lower = (ahead - upper.astype(f32)).astype(bf16)
+            extra.append(
+                (
+                    nt(wide, state_b[c, p, :LANES]) + nt(wide, state_b[c, p, LANES:]),
+                    nt(both, upper) + nt(v, lower[:, :LANES]),
+                )
+            )
+        for p in range(s.pairs):
+            q, k = cut(here, 0, p), cut(here, 1, p)
+            low, high = (part.astype(bf16) * seen for part in raw[p])
+            gq = live * extra[p][0] + nn(
+                jnp.concatenate([low, high], axis=1),
+                jnp.concatenate([k * ones_low, k * ones_high], axis=0),
+            )
+            gk = chosen * extra[p][1] + tn(
+                jnp.concatenate([low, high], axis=0),
+                jnp.concatenate([q * ones_low, q * ones_high], axis=0),
+            )
+            for part, grad in ((0, gq), (1, gk)):
                 grad = grad.astype(bf16)
                 first = part * width + p * LANES
-                if part < 2:
-                    slope = jnp.minimum((q, k)[part].astype(f32), 1.0)
-                    grad = (grad.astype(f32) * slope).astype(bf16)
-                    collect(2, first, grad.astype(f32))
+                slope = jnp.minimum((q, k)[part].astype(f32), 1.0)
+                grad = (grad.astype(f32) * slope).astype(bf16)
+                collect(2, first, grad.astype(f32))
                 act[here, first : first + LANES] = grad
         return carry
 
     lax.fori_loop(0, s.chunks, back_body, 0)
+    projection_grad(0)
+    q_item.start()
+    projection_grad(1)
+    k_item.start()
+    out_item.along()
+    up_item.along_again()
+    q_item.plane()
+    k_item.plane()
+    v_item.along()
+    out_item.along_again()
     down_item.finish()
-    up_item.along()
-    out_item.along()
-
-    for part in range(3):
-        cols = slice(part * width, (part + 1) * width)
-        grad = nn(n1t[...], act[:, cols]).astype(bf16)
-        stage_q[:chips, :, :, cols] = grad.reshape(chips, 2, width // dp, width)
-        qkv_items[part].start()
-    up_item.along_again()
-    out_item.along_again()
-    for item in qkv_items:
-        item.plane()
 
     def input_body(c, carry):
         here = span(c, TALL)
@@ -902,10 +935,9 @@
             )
         )
         vec_back[-1].start()
-    up_item.finish()
-    out_item.finish()
-    for item in qkv_items:
-        item.along()
+    v_item.along_again()
+    q_item.along()
+    k_item.along()
     for copy in vec_back:
         copy.wait_recv()
     total = vstage[me]
@@ -924,8 +956,11 @@
             )
         )
         vec_z[-1].start()
-    for item in qkv_items:
-        item.along_again()
+    q_item.along_again()
+    k_item.along_again()
+    up_item.finish()
+    out_item.finish()
+    v_item.finish()
     for copy in vec_z:
         copy.wait_recv()
     terms = [vz[...]] + [vzback[step] for step in range(seq - 1)]
@@ -933,8 +968,8 @@
         half = len(terms) // 2
         terms = [terms[i] + terms[i + half] for i in range(half)]
     vec_out[...] = terms[0]
-    for item in qkv_items:
-        item.finish()
+    q_item.finish()
+    k_item.finish()
 
     for c in range(rows // TALL):
         here = pl.ds(c * TALL, TALL)
@@ -1017,6 +1052,7 @@
         shapes = [(s.weights[index][0], columns) for index, _, columns in s.scatters]
         dma = pltpu.SemaphoreType.DMA
         tall = s.weights[0][0]
+        message_rows = pairs // 2 * LANES + -(-pairs // 8) * 8
         scratch = (
             [pltpu.VMEM(grid, bf16) for grid in grids]
             + [
@@ -1042,8 +1078,8 @@
                 pltpu.VMEM((dp - 1, 8, s.vec_lanes), f32),
                 pltpu.VMEM((8, s.vec_lanes), f32),
                 pltpu.VMEM((seq - 1, 8, s.vec_lanes), f32),
-                pltpu.VMEM((2, pairs // 2 + 1, LANES, LANES), bf16),
-                pltpu.VMEM((2, seq - 1, pairs // 2 + 1, LANES, LANES), bf16),
+                pltpu.VMEM((2, message_rows, LANES), f32),
+                pltpu.VMEM((2, seq - 1, message_rows, LANES), f32),
                 [pltpu.VMEM((chips,) + shape, bf16) for shape in shapes[:3]],
                 [pltpu.VMEM((nk,) + shape, bf16) for shape in shapes],
                 [pltpu.VMEM(shape, bf16) for shape in shapes],

time: 146 us -> 129 us (0.88)
  Pallas kernels: 145 us -> 128 us
    pallas_call x1, Pallas kernels: 140 us -> 123 us  [body(): pl.pallas_call(functools.partial(kernel, s), out_shape=(jax.ShapeDtypeStr...]
where the time goes in v3:
time: 129 us
  Pallas kernels  128 us (99%)
    pallas_call x1, Pallas kernels, body(): pl.pallas_call(functools.partial(kernel, s), out_shape=(jax.ShapeDtypeStr...  123 us
    pallas_call x1, Pallas kernels, widen(): pl.pallas_call(functools.partial(widen_kernel, parts), out_shape=[jax.Sha...  5.41 us

profile of v3, /device:TPU:0, one launch (start us, length us, event | category | flops | bytes accessed | tf_op | source)
XLA Modules:
  0.0 128.8 jit_solution(15445750063006073965)
XLA Ops:
  0.7 122.6 %layer.1 = (bf16[1280,512]{1,0:T(8,128)(2,1)}, bf16[1280,512]{1,0:T(8,128)(2,1)}, bf16[64,1536]{1,0:T(8,128)(2,1)}, bf16[64,512]{1,0:T(8,128)(2,1)}, bf16[64,204...) custom-call(s32[3]{0:T(128)} %bitcast.23, bf16[1280,512]{1,0:T(8,128)(2,1)} %bitcast.21, ...), custom_call_target="tpu_custom_call" | custom-call | tf_op jit(solution)/shard_map/layer/pallas_call | solution.py:1100
  123.2 5.4 %widen.1 = (bf16[1280,512]{1,0:T(8,128)(2,1)}, f32[1280,512]{1,0:T(8,128)}, f32[64,1536]{1,0:T(8,128)}, f32[64,512]{1,0:T(8,128)}, f32[64,2048]{1,0:T(8,128)}, /...) custom-call(bf16[1280,512]{1,0:T(8,128)(2,1)} %get-tuple-element.35., ...), custom_call_target="tpu_custom_call" | custom-call | tf_op jit(solution)/shard_map/widen/pallas_call | solution.py:1022

commit v4 on v3

--- a/solution.py
+++ b/solution.py
@@ -93,9 +93,8 @@
             (3, 0, w),
             (1, 0, w),
         ) + tuple((2, t * (h // 4), h // 4) for t in range(4))
-        self.scatters = (
+        self.scatters = tuple((2, t * (h // 4), h // 4) for t in range(4)) + (
             (3, 0, w),
-            (2, 0, h),
             (1, 0, w),
             (0, 0, w),
             (0, w, w),
@@ -567,6 +566,173 @@
 
     lax.fori_loop(0, rows // TALL, middle_body, 0)
 
+    outer = (z == 0) | (z == seq - 1)
+    inward = jnp.where(z < seq // 2, z + 1, z - 1)
+    outward = jnp.where(z < seq // 2, z - 1, z + 1)
+    across = seq - 1 - z
+    stages = (stage_q, wo, wu, wd)
+    results = (gq_out, go_out, gu_out, gd_out)
+
+    class Scatter:
+        def __init__(self, item):
+            index, first, columns = s.scatters[item]
+            self.stage, self.result = stages[index], results[index]
+            self.first, self.count, self.height = first, columns, s.weights[index][0]
+            self.cols = pl.ds(first, columns)
+            shared = item - len(s.scatters) + 3
+            self.rb0 = rb0[shared if shared >= 0 else item]
+            self.rb1 = rb1[item]
+            self.zsrc, self.zr1, self.zr2 = zsrc[item], zr1[item], zr2[item]
+            self.part = columns // seq
+            self.short = seq != 4 or item >= len(s.scatters) - 2
+            self.send, self.recv = r_send.at[item], r_recv.at[item]
+
+        def across(self):
+            return remote(
+                self.stage.at[pl.ds(0, chips), 1 - core, :, self.cols],
+                self.rb0,
+                self.send.at[0],
+                self.recv.at[0],
+                sibling,
+            )
+
+        def sends(self):
+            return [
+                remote(
+                    self.stage.at[peer[0] // 2, core, :, self.cols],
+                    self.rb1.at[k],
+                    self.send.at[1 + k],
+                    self.recv.at[1 + k],
+                    peer,
+                )
+                for k, peer in enumerate(peers)
+            ]
+
+        def quarters(self):
+            return [
+                remote(
+                    self.zsrc.at[:, span(lax.rem(z + step, seq), self.part)],
+                    self.zr1.at[pl.ds((step - 1) * self.height, self.height)],
+                    self.send.at[nk + step],
+                    self.recv.at[nk + step],
+                    (me, lax.rem(z + step, seq)),
+                )
+                for step in range(1, seq)
+            ]
+
+        def totals(self, arriving=False):
+            copies = []
+            for step in range(1, seq):
+                owner = lax.rem(z - step + seq, seq) if arriving else z
+                piece = self.zr2.at[:, span(owner, self.part)]
+                k = nk + seq - 1 + step
+                target = (me, lax.rem(z + step, seq))
+                copies.append(remote(piece, piece, self.send.at[k], self.recv.at[k], target))
+            return copies
+
+        def start(self):
+            self.across().start()
+
+        def plane(self):
+            self.across().wait_recv()
+
+            def add(k, carry):
+                here = (k, core, slice(None), self.cols)
+                self.stage[here] = (
+                    self.stage[here].astype(f32) + self.rb0[k].astype(f32)
+                ).astype(bf16)
+                return carry
+
+            lax.fori_loop(0, chips, add, 0)
+            for copy in self.sends():
+                copy.start()
+
+        def along(self):
+            for copy in self.sends():
+                copy.wait_recv()
+            total = self.stage[chip, core, :, self.cols].astype(f32)
+            for k in range(nk):
+                total = total + self.rb1[k].astype(f32)
+            self.zsrc[...] = total.astype(bf16)
+            if self.short:
+                for copy in self.quarters():
+                    copy.start()
+            else:
+
+                @pl.when(outer)
+                def _():
+                    self.step(0).start()
+
+        def step(self, k):
+            source, target = ((self.zsrc, self.zr1), (self.zsrc, self.zr2), (self.zsrc, self.zr2))[k]
+            there = (inward, across, outward)[k]
+            return remote(
+                source, target, self.send.at[nk + 1 + k], self.recv.at[nk + 1 + k], (me, there)
+            )
+
+        def inner(self):
+            @pl.when(jnp.logical_not(outer))
+            def _():
+                self.step(0).wait_recv()
+                total = self.zsrc[...].astype(f32) + self.zr1[...].astype(f32)
+                self.zsrc[...] = total.astype(bf16)
+                self.step(1).start()
+
+        def outward(self):
+            @pl.when(jnp.logical_not(outer))
+            def _():
+                self.step(1).wait()
+                total = self.zsrc[...].astype(f32) + self.zr2[...].astype(f32)
+                self.zsrc[...] = total.astype(bf16)
+                self.step(2).start()
+
+        def along_again(self):
+            for copy in self.quarters():
+                copy.wait_recv()
+            mine = span(z, self.part)
+            total = self.zsrc[:, mine].astype(f32)
+            for step in range(seq - 1):
+                total = total + self.zr1[step * self.height : (step + 1) * self.height].astype(f32)
+            self.zr2[:, mine] = total.astype(bf16)
+            for copy in self.totals():
+                copy.start()
+
+        def finish(self):
+            if self.short:
+                for copy in self.totals(True):
+                    copy.wait_recv()
+                self.result[:, self.cols] = self.zr2[...]
+            else:
+
+                @pl.when(outer)
+                def _():
+                    self.step(2).wait_recv()
+                    self.result[:, self.cols] = self.zr2[...]
+
+                @pl.when(jnp.logical_not(outer))
+                def _():
+                    self.result[:, self.cols] = self.zsrc[...]
+
+        def drain(self):
+            for copy in [self.across()] + self.sends():
+                copy.wait_send()
+            if self.short:
+                for copy in self.quarters() + self.totals():
+                    copy.wait_send()
+            else:
+
+                @pl.when(outer)
+                def _():
+                    self.step(0).wait_send()
+
+                @pl.when(jnp.logical_not(outer))
+                def _():
+                    self.step(2).wait_send()
+
+    scatters = [Scatter(item) for item in range(len(s.scatters))]
+    up_items, down_item, out_item = scatters[:4], scatters[4], scatters[5]
+    q_item, k_item, v_item = scatters[6:]
+
     for t in range(4):
         if t == 1:
             get_up[2].hand_on()
@@ -587,6 +753,19 @@
         total[...] += nn(active, down)
         back = nt(grad, up)
         gmid[...] = back if t == 0 else gmid[...] + back
+        get_up[t].drain()
+        if t == 0:
+            get_down.drain()
+        grad = nn(n2t[...], hgrad[:, :, :, cols].reshape(rows, tile)).astype(bf16)
+        wu[:, :, :, cols] = grad.reshape(chips, 2, width // dp, tile)
+        up_items[t].start()
+        grad = tn(act[:, cols], cot[...]).astype(bf16)
+        wd[t * per : (t + 1) * per] = grad.reshape(per, 2, hidden // dp, width)
+        if t > 0:
+            up_items[t - 1].plane()
+        if t == 3:
+            down_item.start()
+            up_items[0].along()
 
     def output_copy(c):
         here = span(c, TALL)
@@ -604,128 +783,12 @@
         return carry
 
     lax.fori_loop(0, rows // TALL, second_body, 0)
-    for gather in gathers:
+    for gather in gathers[:3] + [get_out]:
         gather.drain()
-
-    stages = (stage_q, wo, wu, wd)
-    results = (gq_out, go_out, gu_out, gd_out)
-
-    class Scatter:
-        def __init__(self, item):
-            index, first, columns = s.scatters[item]
-            self.stage, self.result = stages[index], results[index]
-            self.first, self.count, self.height = first, columns, s.weights[index][0]
-            self.cols = pl.ds(first, columns)
-            shared = item - len(s.scatters) + 3
-            if shared >= 0:
-                self.rb0 = rb0[0].at[:, pl.ds(shared * self.height, self.height)]
-            else:
-                self.rb0 = rb0[item]
-            self.rb1 = rb1[item]
-            self.zsrc, self.zr1, self.zr2 = zsrc[item], zr1[item], zr2[item]
-            self.part = columns // seq
-            self.send, self.recv = r_send.at[item], r_recv.at[item]
-
-        def across(self):
-            return remote(
-                self.stage.at[pl.ds(0, chips), 1 - core, :, self.cols],
-                self.rb0,
-                self.send.at[0],
-                self.recv.at[0],
-                sibling,
-            )
-
-        def sends(self):
-            return [
-                remote(
-                    self.stage.at[peer[0] // 2, core, :, self.cols],
-                    self.rb1.at[k],
-                    self.send.at[1 + k],
-                    self.recv.at[1 + k],
-                    peer,
-                )
-                for k, peer in enumerate(peers)
-            ]
-
-        def quarters(self):
-            return [
-                remote(
-                    self.zsrc.at[:, span(lax.rem(z + step, seq), self.part)],
-                    self.zr1.at[step - 1],
-                    self.send.at[nk + step],
-                    self.recv.at[nk + step],
-                    (me, lax.rem(z + step, seq)),
-                )
-                for step in range(1, seq)
-            ]
-
-        def totals(self, arriving=False):
-            copies = []
-            for step in range(1, seq):
-                owner = lax.rem(z - step + seq, seq) if arriving else z
-                piece = self.zr2.at[:, span(owner, self.part)]
-                k = nk + seq - 1 + step
-                target = (me, lax.rem(z + step, seq))
-                copies.append(remote(piece, piece, self.send.at[k], self.recv.at[k], target))
-            return copies
-
-        def start(self):
-            self.across().start()
-
-        def plane(self):
-            self.across().wait_recv()
-
-            def add(k, carry):
-                here = (k, core, slice(None), self.cols)
-                self.stage[here] = (
-                    self.stage[here].astype(f32) + self.rb0[k].astype(f32)
-                ).astype(bf16)
-                return carry
-
-            lax.fori_loop(0, chips, add, 0)
-            for copy in self.sends():
-                copy.start()
-
-        def along(self):
-            for copy in self.sends():
-                copy.wait_recv()
-            total = self.stage[chip, core, :, self.cols].astype(f32)
-            for k in range(nk):
-                total = total + self.rb1[k].astype(f32)
-            self.zsrc[...] = total.astype(bf16)
-            for copy in self.quarters():
-                copy.start()
-
-        def along_again(self):
-            for copy in self.quarters():
-                copy.wait_recv()
-            mine = span(z, self.part)
-            total = self.zsrc[:, mine].astype(f32)
-            for step in range(seq - 1):
-                total = total + self.zr1[step].astype(f32)
-            self.zr2[:, mine] = total.astype(bf16)
-            for copy in self.totals():
-                copy.start()
-
-        def finish(self):
-            for copy in self.totals(True):
-                copy.wait_recv()
-            self.result[:, self.cols] = self.zr2[...]
-
-        def drain(self):
-            for copy in [self.across()] + self.sends() + self.quarters() + self.totals():
-                copy.wait_send()
-
-    scatters = [Scatter(item) for item in range(len(s.scatters))]
-    down_item, up_item, out_item = scatters[:3]
-
-    def down_body(c, carry):
-        grad = tn(act[:, span(c, tile)], cot[...]).astype(bf16)
-        wd[pl.ds(c * per, per)] = grad.reshape(per, 2, hidden // dp, width)
-        return carry
-
-    lax.fori_loop(0, hidden // tile, down_body, 0)
-    down_item.start()
+    up_items[3].plane()
+    down_item.plane()
+    up_items[1].along()
+    up_items[0].inner()
 
     bd_square = block_diag[:, :LANES].astype(bf16)
     head_sum = jnp.concatenate([bd_square, bd_square], axis=0)
@@ -778,29 +841,68 @@
             state[p] = keep * now + tn(cut(here, 0, p) * live, wide) * block_diag
         return carry
 
-    down_item.plane()
+    up_items[2].along()
+    up_items[1].inner()
+    up_items[0].outward()
     lax.fori_loop(0, s.chunks, gstate_body, 0)
     send_states(1, False)
 
-    def up_body(c, carry):
-        cols = span(c, tile)
-        grad = nn(n2t[...], hgrad[:, :, :, cols].reshape(rows, tile)).astype(bf16)
-        wu[:, :, :, cols] = grad.reshape(chips, 2, width // dp, tile)
-        return carry
-
-    lax.fori_loop(0, hidden // tile, up_body, 0)
-    up_item.start()
     wo[...] = tn(heard[...], gone[...]).astype(bf16).reshape(chips, 2, width // dp, width)
     out_item.start()
-    up_item.plane()
-    out_item.plane()
-
-    q_item, k_item, v_item = scatters[3:]
+    up_items[3].along()
+    up_items[2].inner()
+    up_items[1].outward()
+
+    def keep_grad(here, part, p, grad, feature):
+        first = part * width + p * LANES
+        slope = jnp.minimum(feature.astype(f32), 1.0)
+        grad = (grad.astype(bf16).astype(f32) * slope).astype(bf16)
+        collect(2, first, grad.astype(f32))
+        act[here, first : first + LANES] = grad
+
+    def back_body(c, carry):
+        here = span(c, CHUNK)
+        for at, work in (
+            (0, out_item.plane),
+            (4, down_item.along),
+        ):
+            pl.when(c == min(at, s.chunks - 1))(work)
+        seen = mask[c]
+        live = in_segment(c, before(c))
+        raw = []
+        extra = []
+        for p in range(s.pairs):
+            v = cut(here, 2, p)
+            wide = jnp.concatenate(grads_of(here, p), axis=1)
+            low = jnp.concatenate([v * ones_low, ones_low], axis=1)
+            high = jnp.concatenate([v * ones_high, ones_high], axis=1)
+            raw.append((nt(wide, low), nt(wide, high)))
+            extra.append(nt(wide, state_b[c, p, :LANES]) + nt(wide, state_b[c, p, LANES:]))
+        for p in range(s.pairs):
+            q, k = cut(here, 0, p), cut(here, 1, p)
+            low, high = (part.astype(bf16) * seen for part in raw[p])
+            gq = live * extra[p] + nn(
+                jnp.concatenate([low, high], axis=1),
+                jnp.concatenate([k * ones_low, k * ones_high], axis=0),
+            )
+            first = width + p * LANES
+            acc[here, first : first + LANES] = tn(
+                jnp.concatenate([low, high], axis=0),
+                jnp.concatenate([q * ones_low, q * ones_high], axis=0),
+            )
+            keep_grad(here, 0, p, gq, q)
+        return carry
+
+    lax.fori_loop(0, s.chunks, back_body, 0)
 
     def projection_grad(part):
         cols = slice(part * width, (part + 1) * width)
         grad = nn(n1t[...], act[:, cols]).astype(bf16)
         stage_q[:chips, :, :, cols] = grad.reshape(chips, 2, width // dp, width)
+
+    projection_grad(0)
+    q_item.start()
+
 
     def value_body(c, carry):
         here = span(c, CHUNK)
@@ -818,6 +920,8 @@
         return carry
 
     lax.fori_loop(0, s.chunks, value_body, 0)
+    q_item.plane()
+    out_item.along()
     take_states(1, False)
 
     def ahead_body(c, carry):
@@ -830,79 +934,46 @@
             sums = 2.0 * spread_ends(sums + pltpu.roll(sums, 64, 1)) * block_diag[:, LANES:]
             upper = sums.astype(bf16).astype(f32)
             sums = jnp.where(low_half, upper, sums - upper)
-            state_in[state_at(c, p)] = jnp.concatenate([ahead[:, :LANES], sums], axis=1)
+            ahead = jnp.concatenate([ahead[:, :LANES], sums], axis=1)
+            upper = ahead.astype(bf16)
+            lower = (ahead - upper.astype(f32)).astype(bf16)
+            k, v = cut(here, 1, p), cut(here, 2, p)
+            both = jnp.concatenate([v, jnp.ones_like(v)], axis=1)
+            first = width + p * LANES
+            grad = acc[here, first : first + LANES] + chosen * (
+                nt(both, upper) + nt(v, lower[:, :LANES])
+            )
+            keep_grad(here, 1, p, grad, k)
             grad = acc[here, p * LANES : (p + 1) * LANES] + chosen * nn(
-                cut(here, 1, p), ahead[:, :LANES].astype(bf16)
+                k, upper[:, :LANES]
             )
             first = 2 * width + p * LANES
             act[here, first : first + LANES] = grad.astype(bf16)
         return carry
 
     lax.fori_loop(0, s.chunks, ahead_body, 0)
+    up_items[3].inner()
+    up_items[2].outward()
+    projection_grad(1)
+    k_item.start()
+    down_item.inner()
     projection_grad(2)
     v_item.start()
-    down_item.along()
-
-    def back_body(c, carry):
-        here = span(c, CHUNK)
-        for at, work in ((0, v_item.plane), (2, down_item.along_again), (3, up_item.along)):
-            pl.when(c == min(at, s.chunks - 1))(work)
-        seen = mask[c]
-        live = in_segment(c, before(c))
-        chosen = in_segment(c, ending(c))
-        raw = []
-        extra = []
-        for p in range(s.pairs):
-            v = cut(here, 2, p)
-            wide = jnp.concatenate(grads_of(here, p), axis=1)
-            low = jnp.concatenate([v * ones_low, ones_low], axis=1)
-            high = jnp.concatenate([v * ones_high, ones_high], axis=1)
-            raw.append((nt(wide, low), nt(wide, high)))
-            both = jnp.concatenate([v, jnp.ones_like(v)], axis=1)
-            ahead = state_in[state_at(c, p)]
-            upper = ahead.astype(bf16)
-            lower = (ahead - upper.astype(f32)).astype(bf16)
-            extra.append(
-                (
-                    nt(wide, state_b[c, p, :LANES]) + nt(wide, state_b[c, p, LANES:]),
-                    nt(both, upper) + nt(v, lower[:, :LANES]),
-                )
-            )
-        for p in range(s.pairs):
-            q, k = cut(here, 0, p), cut(here, 1, p)
-            low, high = (part.astype(bf16) * seen for part in raw[p])
-            gq = live * extra[p][0] + nn(
-                jnp.concatenate([low, high], axis=1),
-                jnp.concatenate([k * ones_low, k * ones_high], axis=0),
-            )
-            gk = chosen * extra[p][1] + tn(
-                jnp.concatenate([low, high], axis=0),
-                jnp.concatenate([q * ones_low, q * ones_high], axis=0),
-            )
-            for part, grad in ((0, gq), (1, gk)):
-                grad = grad.astype(bf16)
-                first = part * width + p * LANES
-                slope = jnp.minimum((q, k)[part].astype(f32), 1.0)
-                grad = (grad.astype(f32) * slope).astype(bf16)
-                collect(2, first, grad.astype(f32))
-                act[here, first : first + LANES] = grad
-        return carry
-
-    lax.fori_loop(0, s.chunks, back_body, 0)
-    projection_grad(0)
-    q_item.start()
-    projection_grad(1)
-    k_item.start()
-    out_item.along()
-    up_item.along_again()
-    q_item.plane()
+    out_item.inner()
+    up_items[3].outward()
     k_item.plane()
-    v_item.along()
-    out_item.along_again()
-    down_item.finish()
+    v_item.plane()
+    down_item.outward()
+    q_item.along()
 
     def input_body(c, carry):
         here = span(c, TALL)
+
+        @pl.when(c == 1)
+        def _():
+            q_item.inner()
+            out_item.outward()
+
         grad = nt(act[here, : 3 * width], wq[...].reshape(width, 3 * width))
         hat, scale = normalised(x_ref[here, :].astype(f32))
         collect(0, 0, grad * hat)
@@ -935,9 +1006,9 @@
             )
         )
         vec_back[-1].start()
-    v_item.along_again()
-    q_item.along()
+    q_item.outward()
     k_item.along()
+    v_item.along()
     for copy in vec_back:
         copy.wait_recv()
     total = vstage[me]
@@ -956,11 +1027,10 @@
             )
         )
         vec_z[-1].start()
-    q_item.along_again()
     k_item.along_again()
-    up_item.finish()
-    out_item.finish()
-    v_item.finish()
+    v_item.along_again()
+    for item in scatters[:-2]:
+        item.finish()
     for copy in vec_z:
         copy.wait_recv()
     terms = [vz[...]] + [vzback[step] for step in range(seq - 1)]
@@ -968,8 +1038,8 @@
         half = len(terms) // 2
         terms = [terms[i] + terms[i + half] for i in range(half)]
     vec_out[...] = terms[0]
-    q_item.finish()
     k_item.finish()
+    v_item.finish()
 
     for c in range(rows // TALL):
         here = pl.ds(c * TALL, TALL)
@@ -1051,6 +1121,7 @@
         grids = [(chips, 2) + shape for shape in s.weights]
         shapes = [(s.weights[index][0], columns) for index, _, columns in s.scatters]
         dma = pltpu.SemaphoreType.DMA
+        short = (len(shapes) - 2, len(shapes) - 1) if seq == 4 else range(len(shapes))
         tall = s.weights[0][0]
         message_rows = pairs // 2 * LANES + -(-pairs // 8) * 8
         scratch = (
@@ -1080,10 +1151,13 @@
                 pltpu.VMEM((seq - 1, 8, s.vec_lanes), f32),
                 pltpu.VMEM((2, message_rows, LANES), f32),
                 pltpu.VMEM((2, seq - 1, message_rows, LANES), f32),
-                [pltpu.VMEM((chips,) + shape, bf16) for shape in shapes[:3]],
+                [pltpu.VMEM((chips,) + shape, bf16) for shape in shapes[:-3]],
                 [pltpu.VMEM((nk,) + shape, bf16) for shape in shapes],
                 [pltpu.VMEM(shape, bf16) for shape in shapes],
-                [pltpu.VMEM((seq - 1, tall_, n // seq), bf16) for tall_, n in shapes],
+                [
+                    pltpu.VMEM(((seq - 1) * shape[0], shape[1] // seq) if k in short else shape, bf16)
+                    for k, shape in enumerate(shapes)
+                ],
                 [pltpu.VMEM(shape, bf16) for shape in shapes],
                 dma((len(s.gathers),)),
                 dma((len(s.gathers), nk + 1)),

time: 129 us -> 123 us (0.953)
  Pallas kernels: 128 us -> 122 us
    pallas_call x1, Pallas kernels: 123 us -> 117 us  [body(): pl.pallas_call(functools.partial(kernel, s), out_shape=(jax.ShapeDtypeStr...]
where the time goes in v4:
time: 123 us
  Pallas kernels  122 us (99%)
    pallas_call x1, Pallas kernels, body(): pl.pallas_call(functools.partial(kernel, s), out_shape=(jax.ShapeDtypeStr...  117 us
    pallas_call x1, Pallas kernels, widen(): pl.pallas_call(functools.partial(widen_kernel, parts), out_shape=[jax.Sha...  5.41 us

profile of v4, /device:TPU:0, one launch (start us, length us, event | category | flops | bytes accessed | tf_op | source)
XLA Modules:
  0.0 123.2 jit_solution(13987310927281627150)
XLA Ops:
  0.7 117.0 %layer.1 = (bf16[1280,512]{1,0:T(8,128)(2,1)}, bf16[1280,512]{1,0:T(8,128)(2,1)}, bf16[64,1536]{1,0:T(8,128)(2,1)}, bf16[64,512]{1,0:T(8,128)(2,1)}, bf16[64,204...) custom-call(s32[3]{0:T(128)} %bitcast.23, bf16[1280,512]{1,0:T(8,128)(2,1)} %bitcast.21, ...), custom_call_target="tpu_custom_call" | custom-call | tf_op jit(solution)/shard_map/layer/pallas_call | solution.py:1174
  117.6 5.4 %widen.1 = (bf16[1280,512]{1,0:T(8,128)(2,1)}, f32[1280,512]{1,0:T(8,128)}, f32[64,1536]{1,0:T(8,128)}, f32[64,512]{1,0:T(8,128)}, f32[64,2048]{1,0:T(8,128)}, /...) custom-call(bf16[1280,512]{1,0:T(8,128)(2,1)} %get-tuple-element.35., ...), custom_call_target="tpu_custom_call" | custom-call | tf_op jit(solution)/shard_map/widen/pallas_call | solution.py:1092

commit v5 on v4

--- a/solution.py
+++ b/solution.py
@@ -765,7 +765,6 @@
             up_items[t - 1].plane()
         if t == 3:
             down_item.start()
-            up_items[0].along()
 
     def output_copy(c):
         here = span(c, TALL)
@@ -787,8 +786,8 @@
         gather.drain()
     up_items[3].plane()
     down_item.plane()
+    up_items[0].along()
     up_items[1].along()
-    up_items[0].inner()
 
     bd_square = block_diag[:, :LANES].astype(bf16)
     head_sum = jnp.concatenate([bd_square, bd_square], axis=0)
@@ -841,17 +840,17 @@
             state[p] = keep * now + tn(cut(here, 0, p) * live, wide) * block_diag
         return carry
 
+    up_items[0].inner()
+    up_items[1].inner()
     up_items[2].along()
-    up_items[1].inner()
-    up_items[0].outward()
     lax.fori_loop(0, s.chunks, gstate_body, 0)
     send_states(1, False)
 
     wo[...] = tn(heard[...], gone[...]).astype(bf16).reshape(chips, 2, width // dp, width)
     out_item.start()
+    up_items[0].outward()
+    up_items[1].outward()
     up_items[3].along()
-    up_items[2].inner()
-    up_items[1].outward()
 
     def keep_grad(here, part, p, grad, feature):
         first = part * width + p * LANES
@@ -952,14 +951,15 @@
         return carry
 
     lax.fori_loop(0, s.chunks, ahead_body, 0)
+    up_items[2].inner()
     up_items[3].inner()
-    up_items[2].outward()
     projection_grad(1)
     k_item.start()
     down_item.inner()
     projection_grad(2)
     v_item.start()
     out_item.inner()
+    up_items[2].outward()
     up_items[3].outward()
     k_item.plane()
     v_item.plane()

time: 123 us -> 126 us (1.024)
  Pallas kernels: 122 us -> 125 us
    pallas_call x1, Pallas kernels: 117 us -> 119 us  [body(): pl.pallas_call(functools.partial(kernel, s), out_shape=(jax.ShapeDtypeStr...]
where the time goes in v5:
time: 126 us; the launch traced here: 125 us
  Pallas kernels  125 us (99%)
    pallas_call x1, Pallas kernels, body(): pl.pallas_call(functools.partial(kernel, s), out_shape=(jax.ShapeDtypeStr...  119 us
    pallas_call x1, Pallas kernels, widen(): pl.pallas_call(functools.partial(widen_kernel, parts), out_shape=[jax.Sha...  5.41 us

profile of v5, /device:TPU:0, one launch (start us, length us, event | category | flops | bytes accessed | tf_op | source)
XLA Modules:
  0.0 125.5 jit_solution(14076307546339203084)
XLA Ops:
  0.7 119.2 %layer.1 = (bf16[1280,512]{1,0:T(8,128)(2,1)}, bf16[1280,512]{1,0:T(8,128)(2,1)}, bf16[64,1536]{1,0:T(8,128)(2,1)}, bf16[64,512]{1,0:T(8,128)(2,1)}, bf16[64,204...) custom-call(s32[3]{0:T(128)} %bitcast.23, bf16[1280,512]{1,0:T(8,128)(2,1)} %bitcast.21, ...), custom_call_target="tpu_custom_call" | custom-call | tf_op jit(solution)/shard_map/layer/pallas_call | solution.py:1174
  119.9 5.4 %widen.1 = (bf16[1280,512]{1,0:T(8,128)(2,1)}, f32[1280,512]{1,0:T(8,128)}, f32[64,1536]{1,0:T(8,128)}, f32[64,512]{1,0:T(8,128)}, f32[64,2048]{1,0:T(8,128)}, /...) custom-call(bf16[1280,512]{1,0:T(8,128)(2,1)} %get-tuple-element.35., ...), custom_call_target="tpu_custom_call" | custom-call | tf_op jit(solution)/shard_map/widen/pallas_call | solution.py:1092
